TPU v7x, 512 devices: a whole 4x8x8 slice. The times are simulated.
512 devices in a mesh: dp: 64 (over y, z), mp: 8 (over x, core).
Axes of the slice: x: 4, y: 8, z: 8, core: 2. Of those that a mesh axis runs over, the one named last changes fastest.
Arguments:
- activations: bfloat16 [16384, 4096], P('dp', 'mp'), may hold values from -6 to 6
- out_grad: bfloat16 [16384, 14336], P('dp', 'mp'), may hold values from -6 to 6
- row_blocks: int32 [112, 8], P('mp'), may hold values from 0 to 31, as said below
- doc_lengths: int32 [64, 4], P('dp'), may hold values from 0 to 256, as said below
Outputs:
- weight_grad: float32 [112, 1024, 128], P('mp', 'dp')
Inputs may be any that keep to these rules, and one draw needn't show every extreme that they name: `row_blocks`: each row holds 8 distinct row-block indices. `doc_lengths`: the lengths of one index of dp sum to at most 256; at some index one document fills all 256 slots.
All inputs are finite; a program needn't handle non-finite values.
Results may differ from a plain program's by a relative error of at most 0.0003.
Values may be sent and summed in bfloat16 or wider, within the bound.
A program may use at most 64 MiB of HBM per device.

v0:
```python
import jax
import jax.numpy as jnp
from jax import lax
from jax.sharding import PartitionSpec as P

BLOCK = 128


def block_sums(features, grads, row_blocks, width):
    slot_count = features.shape[0]
    blocked = features.reshape(slot_count, features.shape[1] // width, width)
    column_count = grads.shape[1] // width

    def one_column(column):
        chosen = jnp.take(blocked, row_blocks[column], axis=1).reshape(slot_count, -1)
        piece = lax.dynamic_slice_in_dim(grads, column * width, width, 1)
        return lax.dot_general(
            chosen, piece, (((0,), (0,)), ((), ())), preferred_element_type=jnp.float32
        )

    return lax.map(one_column, jnp.arange(column_count, dtype=jnp.int32))


def shards(activations, out_grad, row_blocks, doc_lengths):
    features = lax.all_gather(activations, "mp", axis=1, tiled=True)
    slot_count = features.shape[0]
    width = BLOCK
    live = jnp.sum(doc_lengths)
    slots = jnp.arange(slot_count, dtype=jnp.int32)
    masked = jnp.where((slots < live)[:, None], out_grad, jnp.zeros_like(out_grad))
    partial_sums = block_sums(features, masked, row_blocks, width)
    total_slots = slot_count * lax.axis_size("dp")
    partial_sums = partial_sums * (jnp.float32(1.0) / jnp.sqrt(jnp.float32(total_slots)))
    owners = lax.axis_size("dp")
    column_count = partial_sums.shape[0]
    stacked = partial_sums.shape[1]
    pieces = partial_sums.reshape(column_count, owners, stacked // owners, width)
    received = lax.all_to_all(pieces, "dp", split_axis=1, concat_axis=1, tiled=True)
    return jnp.sum(received, axis=1)


def solution(mesh):
    in_specs = (P("dp", "mp"), P("dp", "mp"), P("mp", None), P("dp", None))
    out_specs = P("mp", "dp", None)
    return jax.shard_map(shards, mesh=mesh, in_specs=in_specs, out_specs=out_specs, check_vma=False)
```

profile of v0, /device:TPU:46, one launch (start us, length us, event | category | flops | bytes accessed | tf_op | source)
XLA Modules:
  0.0 371.4 jit_solution(16793028514108389227)
XLA Ops:
  6.5 1.8 copy.16
  8.4 1.3 reduce_sum.18
  9.7 0.8 copy.17
  10.5 0.6 iota_compare_fusion
  11.1 2.2 broadcast_select_fusion
  13.3 29.9 %all-gather.2.cloned.1.call-done = bf16[256,4096]{0,1:T(8,128)(2,1)} async-done(((bf16[256,512]{0,1:T(8,128)(2,1)}), bf16[256,4096]{0,1:T(8,128)(2,1)}) %all-gather.2.cloned.1.call-update) | async-done | bytes 2097168 | tf_op jit(solution)/shard_map/all_gather | solution.py:25
  43.2 3.2 copy.18
  46.5 92.3 %while.10 = (s32[]{:T(128)}, f32[14,1024,128]{2,1,0:T(8,128)}, s32[14]{0:T(128)S(1)}, s32[14,8]{1,0:T(8,128)S(1)}, bf16[256,32,128]{2,0,1:T(8,128)(2,1)S(1)}, /*...) while((s32[]{:T(128)}, f32[14,1024,128]{2,1,0:T(8,128)}, ...), condition=%wide.region_2.3_spmd, body=%wide.region_1.2_spmd.sunk | while | flops 67372112 | bytes 4266885 | solution.py:21
  46.5 0.7 dynamic_slice.24
  49.2 0.6 gather_fusion
  49.9 0.2 copy.21
  51.1 1.9 fusion.12
  53.1 0.7 dynamic_slice.24
  55.8 0.6 gather_fusion
  56.5 0.2 copy.21
  57.7 2.0 fusion.12
  59.7 0.7 dynamic_slice.24
  62.4 0.6 gather_fusion
  63.1 0.2 copy.21
  64.3 2.0 fusion.12
  66.3 0.7 dynamic_slice.24
  69.0 0.6 gather_fusion
  69.7 0.2 copy.21
  70.9 2.0 fusion.12
  72.9 0.7 dynamic_slice.24
  75.6 0.6 gather_fusion
  76.3 0.2 copy.21
  77.5 1.9 fusion.12
  79.4 0.7 dynamic_slice.24
  82.2 0.6 gather_fusion
  82.9 0.2 copy.21
  84.1 1.9 fusion.12
  86.0 0.7 dynamic_slice.24
  88.8 0.6 gather_fusion
  90.7 1.9 fusion.12
  92.6 0.7 dynamic_slice.24
  95.4 0.6 gather_fusion
  96.0 0.2 copy.21
  97.3 2.0 fusion.12
  99.2 0.7 dynamic_slice.24
  102.0 0.6 gather_fusion
  102.6 0.2 copy.21
  103.9 1.9 fusion.12
  105.8 0.7 dynamic_slice.24
  108.6 0.6 gather_fusion
  109.2 0.2 copy.21
  110.4 2.0 fusion.12
  112.4 0.7 dynamic_slice.24
  115.2 0.6 gather_fusion
  115.8 0.2 copy.21
  117.1 1.9 fusion.12
  119.0 0.7 dynamic_slice.24
  121.8 0.6 gather_fusion
  123.6 2.0 fusion.12
  125.6 0.7 dynamic_slice.24
  128.4 0.6 gather_fusion
  130.2 1.9 fusion.12
  132.2 0.7 dynamic_slice.24
  135.0 0.6 gather_fusion
  136.8 2.0 fusion.12
  138.8 3.7 broadcast_multiply_fusion
  142.5 1.1 copy.19
  143.6 216.8 %all_to_all.5 = f32[14,64,16,128]{3,2,0,1:T(8,128)} all-to-all(f32[14,64,16,128]{3,2,0,1:T(8,128)S(1)} %copy.19), channel_id=1, replica_groups=mesh['dp'=64,'mp'=8] {'dp'}, dimensions={1} | all-to-all | bytes 14680064 | tf_op jit(solution)/shard_map/all_to_all | solution.py:38
  360.4 4.2 %reduce_sum.19 = f32[14,16,128]{2,1,0:T(8,128)} reduce(f32[14,64,16,128]{3,2,0,1:T(8,128)} %all_to_all.5, f32[]{:T(128)} %constant.29.clone.1), dimensions={1}, to_apply=%region_3.4 | reduce | flops 1806336 | bytes 7454724 | tf_op jit(solution)/shard_map/reduce_sum | solution.py:39
  (78 shorter events, 5.3 us)
Async XLA Ops:
  6.5 36.7 %all-gather.2.cloned.1.call-start = ((), (), s32[]{:S(2)}) async-start(), calls=%async_computation.1 | async-start | bytes 2359296 | tf_op jit(solution)/shard_map/all_gather | solution.py:25
Sparse Core Ops, SparseCore 0:
  9.5 33.6 all-gather.1
where the time goes:
time: 373 us; the launch traced here: 371 us
  blocking collectives  217 us (58%)
  loops' own time  39.3 us (11%)
  waiting for transfers between devices  29.9 us (8%)
  local copies, waits for them, and re-layouts  29.2 us (8%)
  matrix products  27.3 us (7%)
  other arithmetic  15.5 us (4%)
  between operations  13.4 us (4%)
    all_to_all x1, blocking collectives, shards(): lax.all_to_all(pieces, 'dp', split_axis=1, concat_axis=1, tiled=True)  217 us
    another operation x1, loops' own time, block_sums(): return lax.map(one_column, jnp.arange(column_count, dtype=jnp.int32))  39.3 us
    all_gather x1, waiting for transfers between devices, shards(): features = lax.all_gather(activations, 'mp', axis=1, tiled=True)  29.9 us
    dot_general x14, matrix products, one_column(): lax.dot_general(chosen, piece, (((0,), (0,)), ((), ())), preferred_elemen...  27.3 us
    gather x28, local copies, waits for them, and re-layouts, one_column(): jnp.take(blocked, row_blocks[column], axis=1).reshape(slot_count, -1)  12.1 us
    dynamic_slice x14, local copies, waits for them, and re-layouts, block_sums(): return lax.map(one_column, jnp.arange(column_count, dtype=jnp.int32))  9.27 us
  transfers between devices with their start and end apart: 1, of which 1 were waited for; matrix products, arithmetic and copies ran while one was open for 1% of the time, Pallas kernels for 0%

commit v1 on v0

v1 whole, which is shorter than its diff:
```python
import functools
import math

import jax
import jax.numpy as jnp
from jax import lax
from jax.experimental import pallas as pl
from jax.experimental.pallas import tpu as pltpu
from jax.sharding import PartitionSpec as P

BLOCK = 128
CORES = 2
TOP = 32700.0
TINY = 1e-33


def quantize(x):
    peak = jnp.maximum(jnp.max(jnp.abs(x), axis=0, keepdims=True), TINY)
    return jnp.round(x * (TOP / peak)).astype(jnp.int32).astype(jnp.int16), peak * (1.0 / TOP)


def widen(q, scale):
    return q.astype(jnp.int32).astype(jnp.float32) * scale


def kernel(cfg, act, grad, rb, docs, out, feat, gm, sbuf, rbuf, ssc, rsc, s2buf, r2buf, s2sc, r2sc, fin,
           sib_s, sib_r, x_s, x_r, d_s, d_r, c_s, c_r, d2_s, d2_r, c2_s, c2_r):
    (ny, nz, nx, nb, knz, per_half, groups, factor) = cfg
    slots = act.shape[0]
    dp = lax.axis_index("dp")
    mp = lax.axis_index("mp")
    at = (dp // nz, lax.rem(dp, nz))
    sizes = (ny, nz)
    x, core = mp // CORES, lax.rem(mp, CORES)
    sibling = x * CORES + (1 - core)

    def along(axis, step):
        there = lax.rem(at[axis] + step + sizes[axis], sizes[axis])
        if axis == 0:
            return {"dp": there * nz + at[1], "mp": mp}
        return {"dp": at[0] * nz + there, "mp": mp}

    def x_device(step):
        return lax.rem(x + step + nx, nx) * CORES + core

    peers = [{"dp": dp, "mp": sibling}]
    if nx > 1:
        peers += [{"dp": dp, "mp": x_device(1)}, {"dp": dp, "mp": x_device(-1)}]
    for axis in (0, 1):
        peers += [along(axis, t) for t in range(1, sizes[axis])]
    barrier = pltpu.get_barrier_semaphore()
    for peer in peers:
        pl.semaphore_signal(barrier, inc=1, device_id=peer, device_id_type=pl.DeviceIdType.MESH)

    for b in range(nb):
        feat[mp * nb + b] = act[:, b * BLOCK:(b + 1) * BLOCK].T
    pl.semaphore_wait(barrier, len(peers))

    half = nb // 2

    def piece(device, part):
        return feat.at[pl.ds(device * nb + part * half, half)]

    def push(device, part, to, send, recv):
        return pltpu.make_async_remote_copy(
            src_ref=piece(device, part), dst_ref=piece(device, part), send_sem=send, recv_sem=recv,
            device_id={"dp": dp, "mp": to}, device_id_type=pl.DeviceIdType.MESH)

    def share(hop, device, part):
        return push(device, part, sibling, sib_s.at[hop, part], sib_r.at[hop, part])

    started = []

    def go(copy):
        copy.start()
        started.append(copy)

    if nx > 1:
        right, left, far = x_device(1), x_device(-1), x_device(2)
        go(push(mp, 0, right, x_s.at[0, 0], x_r.at[0, 0]))
        go(push(mp, 1, left, x_s.at[1, 0], x_r.at[1, 0]))
        go(push(mp, 1, right, x_s.at[0, 1], x_r.at[0, 1]))
        go(push(mp, 0, left, x_s.at[1, 1], x_r.at[1, 1]))
    go(share(0, mp, 0))
    go(share(0, mp, 1))

    live = docs[0, 0]
    for d in range(1, docs.shape[1]):
        live = live + docs[0, d]
    keep = lax.broadcasted_iota(jnp.int32, (slots, BLOCK), 0) < live
    for c in range(2 * per_half):
        part = grad[:, c * BLOCK:(c + 1) * BLOCK]
        gm[c] = jnp.where(keep, part, jnp.zeros_like(part))

    if nx > 1:
        push(left, 0, right, x_s.at[0, 0], x_r.at[0, 0]).wait_recv()
        go(push(left, 0, right, x_s.at[0, 2], x_r.at[0, 2]))
        go(share(1, left, 0))
        push(right, 1, left, x_s.at[1, 0], x_r.at[1, 0]).wait_recv()
        go(push(right, 1, left, x_s.at[1, 2], x_r.at[1, 2]))
        go(share(2, right, 1))
        push(left, 1, right, x_s.at[0, 1], x_r.at[0, 1]).wait_recv()
        go(share(1, left, 1))
        push(right, 0, left, x_s.at[1, 1], x_r.at[1, 1]).wait_recv()
        go(share(2, right, 0))
        push(far, 0, right, x_s.at[0, 2], x_r.at[0, 2]).wait_recv()
        go(share(3, far, 0))
        push(far, 1, left, x_s.at[1, 2], x_r.at[1, 2]).wait_recv()
        go(share(3, far, 1))
    for hop in range(4 if nx > 1 else 1):
        for part in (0, 1):
            share(hop, mp, part).wait_recv()

    rows = BLOCK // nz if nz > 1 else BLOCK // 1
    sub = (BLOCK // nz, BLOCK // ny)

    def local(h, c, owner):
        if h == 0:
            lhs = feat[rb[c, owner]]
        else:
            span = BLOCK // nz
            lhs = jnp.concatenate(
                [feat[rb[per_half + c, k], pl.ds(pl.multiple_of(owner * span, span), span), :] for k in range(knz)], axis=0)
        return jnp.dot(lhs, gm[h * per_half + c], preferred_element_type=jnp.float32)

    def message(h, way, s, g):
        lo, hi = groups[g]
        n = sizes[h]
        where = pl.ds(0, BLOCK)
        if s == 0:
            where = pl.ds(way * (BLOCK // 2), BLOCK // 2)
        to = along(h, 1 - 2 * way)
        data = pltpu.make_async_remote_copy(
            src_ref=sbuf.at[h, way, s, pl.ds(lo, hi - lo), where], dst_ref=rbuf.at[h, way, s, pl.ds(lo, hi - lo), where],
            send_sem=d_s.at[h, way, s, g], recv_sem=d_r.at[h, way, s, g],
            device_id=to, device_id_type=pl.DeviceIdType.MESH)
        scale = pltpu.make_async_remote_copy(
            src_ref=ssc.at[h, way, s, g], dst_ref=rsc.at[h, way, s, g],
            send_sem=c_s.at[h, way, s, g], recv_sem=c_r.at[h, way, s, g],
            device_id=to, device_id_type=pl.DeviceIdType.MESH)
        return data, scale

    def arrived(h, way, s, g):
        for copy in message(h, way, s, g):
            copy.wait_recv()

    def add_arrived(x, h, way, s, g, c):
        lo = groups[g][0]
        scale = rsc[h, way, s, g, pl.ds(c - lo, 1), :]
        if s > 0:
            return x + widen(rbuf[h, way, s, c], scale)
        mid = BLOCK // 2
        here = widen(rbuf[h, way, s, c, pl.ds(way * mid, mid), :], scale)
        if way == 0:
            return jnp.concatenate([x[:mid] + here, x[mid:]], axis=0)
        return jnp.concatenate([x[:mid], x[mid:] + here], axis=0)

    def first_step(h, g):
        lo, hi = groups[g]
        n = sizes[h]
        owner = lax.rem(at[h] + n // 2, n)

        def column(c, _):
            x = local(h, c, owner)
            mid = BLOCK // 2
            for way in (0, 1):
                q, scale = quantize(x[way * mid:(way + 1) * mid])
                sbuf[h, way, 0, c, pl.ds(way * mid, mid), :] = q
                ssc[h, way, 0, g, pl.ds(c - lo, 1), :] = scale
            return 0
        lax.fori_loop(lo, hi, column, 0)
        for way in (0, 1):
            for copy in message(h, way, 0, g):
                go(copy)

    def later_step(h, way, s, g):
        lo, hi = groups[g]
        n = sizes[h]
        distance = n // 2 - s
        owner = lax.rem(at[h] + (1 - 2 * way) * distance + n, n)
        arrived(h, way, s - 1, g)

        def column(c, _):
            x = add_arrived(local(h, c, owner), h, way, s - 1, g, c)
            q, scale = quantize(x)
            sbuf[h, way, s, c] = q
            ssc[h, way, s, g, pl.ds(c - lo, 1), :] = scale
            return 0
        lax.fori_loop(lo, hi, column, 0)
        for copy in message(h, way, s, g):
            go(copy)

    def second(h, t, g):
        lo, hi = groups[g]
        axis = 1 - h
        to = along(axis, t)
        there = lax.rem(at[axis] + t, sizes[axis])
        data = pltpu.make_async_remote_copy(
            src_ref=s2buf.at[h, there, pl.ds(lo, hi - lo)], dst_ref=r2buf.at[h, t, pl.ds(lo, hi - lo)],
            send_sem=d2_s.at[h, t, g], recv_sem=d2_r.at[h, t, g],
            device_id=to, device_id_type=pl.DeviceIdType.MESH)
        scale = pltpu.make_async_remote_copy(
            src_ref=s2sc.at[h, g], dst_ref=r2sc.at[h, t, g],
            send_sem=c2_s.at[h, t, g], recv_sem=c2_r.at[h, t, g],
            device_id=to, device_id_type=pl.DeviceIdType.MESH)
        return data, scale

    def own_step(h, g):
        lo, hi = groups[g]
        n = sizes[h]
        last = n // 2 - 1
        if n > 1:
            for way in (0, 1):
                arrived(h, way, last, g)

        def column(c, _):
            x = local(h, c, at[h])
            if n > 1:
                for way in (0, 1):
                    x = add_arrived(x, h, way, last, g, c)
            fin[h, c] = x
            q, scale = quantize(x)
            span = BLOCK // sizes[1 - h]
            for o in range(sizes[1 - h]):
                s2buf[h, o, c] = q[o * span:(o + 1) * span]
            s2sc[h, g, pl.ds(c - lo, 1), :] = scale
            return 0
        lax.fori_loop(lo, hi, column, 0)
        for t in range(1, sizes[1 - h]):
            for copy in second(h, t, g):
                go(copy)

    def finish(h, g):
        lo, hi = groups[g]
        n = sizes[1 - h]
        span = BLOCK // n
        for t in range(1, n):
            for copy in second(h, t, g):
                copy.wait_recv()

        def column(c, _):
            x = fin[h, c, pl.ds(pl.multiple_of(at[1 - h] * span, span), span), :]
            for t in range(1, n):
                x = x + widen(r2buf[h, t, c], r2sc[h, t, g, pl.ds(c - lo, 1), :])
            out[h * per_half + c] = x * factor
            return 0
        lax.fori_loop(lo, hi, column, 0)

    for s in range(max(sizes) // 2):
        for g in range(len(groups)):
            for h in (0, 1):
                if s >= sizes[h] // 2:
                    continue
                if s == 0:
                    first_step(h, g)
                else:
                    for way in (0, 1):
                        later_step(h, way, s, g)
    for g in range(len(groups)):
        for h in (0, 1):
            own_step(h, g)
    for g in range(len(groups)):
        for h in (0, 1):
            finish(h, g)
    for copy in started:
        copy.wait_send()


def shards(ny, nz, nx, groups, activations, out_grad, row_blocks, doc_lengths):
    slots = activations.shape[0]
    nb = activations.shape[1] // BLOCK
    columns, knz = row_blocks.shape
    per_half = columns // 2
    dp = ny * nz
    factor = 1.0 / math.sqrt(slots * dp)
    cfg = (ny, nz, nx, nb, knz, per_half, groups, factor)
    blocks = nb * nx * CORES
    steps = max(1, max(ny, nz) // 2)
    ng = len(groups)
    span = BLOCK // min(ny, nz)
    most = max(ny, nz)
    vmem = pl.BlockSpec(memory_space=pltpu.VMEM)
    smem = pl.BlockSpec(memory_space=pltpu.SMEM)
    dma = pltpu.SemaphoreType.DMA
    return pl.pallas_call(
        functools.partial(kernel, cfg),
        out_shape=jax.ShapeDtypeStruct((columns, knz * BLOCK // dp, BLOCK), jnp.float32),
        in_specs=[vmem, vmem, smem, smem],
        out_specs=vmem,
        scratch_shapes=[
            pltpu.VMEM((blocks, BLOCK, slots), jnp.bfloat16),
            pltpu.VMEM((columns, slots, BLOCK), jnp.bfloat16),
            pltpu.VMEM((2, 2, steps, per_half, BLOCK, BLOCK), jnp.int16),
            pltpu.VMEM((2, 2, steps, per_half, BLOCK, BLOCK), jnp.int16),
            pltpu.VMEM((2, 2, steps, ng, 8, BLOCK), jnp.float32),
            pltpu.VMEM((2, 2, steps, ng, 8, BLOCK), jnp.float32),
            pltpu.VMEM((2, most, per_half, span, BLOCK), jnp.int16),
            pltpu.VMEM((2, most, per_half, span, BLOCK), jnp.int16),
            pltpu.VMEM((2, ng, 8, BLOCK), jnp.float32),
            pltpu.VMEM((2, most, ng, 8, BLOCK), jnp.float32),
            pltpu.VMEM((2, per_half, BLOCK, BLOCK), jnp.float32),
            dma((4, 2)), dma((4, 2)),
            dma((2, 3)), dma((2, 3)),
            dma((2, 2, steps, ng)), dma((2, 2, steps, ng)),
            dma((2, 2, steps, ng)), dma((2, 2, steps, ng)),
            dma((2, most, ng)), dma((2, most, ng)),
            dma((2, most, ng)), dma((2, most, ng)),
        ],
        compiler_params=pltpu.CompilerParams(
            collective_id=0, has_side_effects=True, vmem_limit_bytes=40 * 2**20),
    )(activations, out_grad, row_blocks, doc_lengths)


def solution(mesh):
    dp, mp = mesh.shape["dp"], mesh.shape["mp"]
    nz = math.isqrt(dp)
    ny = dp // nz
    body = functools.partial(shards, ny, nz, mp // CORES, ((0, 2), (2, 4), (4, 7)))
    in_specs = (P("dp", "mp"), P("dp", "mp"), P("mp", None), P("dp", None))
    return jax.shard_map(body, mesh=mesh, in_specs=in_specs, out_specs=P("mp", "dp", None), check_vma=False)
```

time: 373 us -> 66.3 us (0.18)
  the two profiles are of different devices: /device:TPU:46 before, /device:TPU:1 now
where the time goes in v1:
time: 66.3 us; the launch traced here: 66.1 us
  Pallas kernels  62.6 us (94%)
  local copies, waits for them, and re-layouts  3.56 us (5%)
    pallas_call x1, Pallas kernels, shards(): pl.pallas_call(functools.partial(kernel, cfg), out_shape=jax.ShapeDtypeSt...  62.6 us
    unnamed x8, local copies, waits for them, and re-layouts  3.56 us

profile of v1, /device:TPU:1, one launch (start us, length us, event | category | flops | bytes accessed | tf_op | source)
XLA Modules:
  0.0 66.1 jit_solution(668771114112237066)
XLA Ops:
  0.0 0.0 copy-start.2
  0.0 0.8 %copy.5.rb = s32[14,8]{1,0:T(8,128)S(1)} copy(s32[14,8]{0,1:T(8,128)} %param.6) | data formatting | bytes 896 | tf_op args[2]
  0.8 0.0 copy-done.2
  0.8 0.0 copy-start
  0.8 1.2 %copy-done = bf16[256,1792]{1,0:T(8,128)(2,1)S(1)} copy-done((bf16[256,1792]{1,0:T(8,128)(2,1)S(1)}, bf16[256,1792]{1,0:T(8,128)(2,1)}, u32[]{:S(2)}) %copy-start) | copy-done | bytes 917528
  2.0 0.0 copy-start.1
  2.0 0.9 %copy-done.1 = bf16[256,512]{1,0:T(8,128)(2,1)S(1)} copy-done((bf16[256,512]{1,0:T(8,128)(2,1)S(1)}, bf16[256,512]{1,0:T(8,128)(2,1)}, u32[]{:S(2)}) %copy-start.1) | copy-done | bytes 262168
  2.9 62.6 %shard_map.46 = f32[14,16,128]{2,1,0:T(8,128)S(1)} custom-call(bf16[256,512]{1,0:T(8,128)(2,1)S(1)} %copy-done.1, bf16[256,1792]{1,0:T(8,128)(2,1)S(1)} %copy-done, s32[14,8]{1,0:T(8,128)S(1)} %copy.5.rb, s32[1,4]{1,0:T(1,128)S(1)} %copy-done.2), custom_call_target="tpu_custom_call" | custom-call | tf_op jit(solution)/shard_map/pallas_call | solution.py:285
  65.5 0.6 copy.7
Async XLA Ops:
  0.0 0.8 %copy-start.2 = (s32[1,4]{1,0:T(1,128)S(1)}, s32[1,4]{1,0:T(1,128)}, u32[]{:S(2)}) copy-start(s32[1,4]{1,0:T(1,128)} %docs.1) | copy-start | bytes 52
  0.8 1.2 %copy-start = (bf16[256,1792]{1,0:T(8,128)(2,1)S(1)}, bf16[256,1792]{1,0:T(8,128)(2,1)}, u32[]{:S(2)}) copy-start(bf16[256,1792]{1,0:T(8,128)(2,1)} %grad.1) | copy-start | bytes 2752516
  2.0 0.9 %copy-start.1 = (bf16[256,512]{1,0:T(8,128)(2,1)S(1)}, bf16[256,512]{1,0:T(8,128)(2,1)}, u32[]{:S(2)}) copy-start(bf16[256,512]{1,0:T(8,128)(2,1)} %act.1) | copy-start | bytes 786436

commit v2 on v0

v2 whole, which is shorter than its diff:
```python
import functools
import math

import jax
import jax.numpy as jnp
from jax import lax
from jax.experimental import pallas as pl
from jax.experimental.pallas import tpu as pltpu
from jax.sharding import PartitionSpec as P

BLOCK = 128
CORES = 2
CODES = 16
FINE = 64.0
TOP = 32700.0
TINY = 1e-33
GROUPS = ((0, 2), (2, 4), (4, 7))
MESH = pl.DeviceIdType.MESH


def quantize(x):
    peak = jnp.maximum(jnp.max(jnp.abs(x), axis=0, keepdims=True), TINY)
    code = jnp.ceil(jnp.log2(peak * (1.0 / TOP)) * FINE)
    q = jnp.round(x * jnp.exp2(code * (-1.0 / FINE)))
    return q.astype(jnp.int32).astype(jnp.int16), code


def code_rows(codes):
    rows = jnp.concatenate(codes + [jnp.zeros((CODES - len(codes), BLOCK), jnp.float32)], axis=0)
    return rows.astype(jnp.int32).astype(jnp.int16)


def scales_of(tile):
    return jnp.exp2(tile.astype(jnp.int32).astype(jnp.float32) * (1.0 / FINE))


def widen(q, scale):
    return q.astype(jnp.int32).astype(jnp.float32) * scale


def first_way(g):
    return 1 if g == len(GROUPS) - 1 else 0


def kernel(cfg, act_hbm, grad_hbm, rb_hbm, docs_hbm, out, act, grad, rb, docs, feat, gm, part, sn, rn, s2, r2, c2, rc2, fin,
           in_sem, x_r, sib_r, m_r, m2_r, send_sem):
    n, nx, nb, knz, per_half, groups, factor = cfg
    slots = act.shape[0]
    span = BLOCK // n
    steps = n // 2
    dp = lax.axis_index("dp")
    mp = lax.axis_index("mp")
    at = (dp // n, lax.rem(dp, n))
    x, core = mp // CORES, lax.rem(mp, CORES)
    sibling = x * CORES + (1 - core)

    def along(axis, step):
        there = lax.rem(at[axis] + step + n, n)
        if axis == 0:
            return {"dp": there * n + at[1], "mp": mp}
        return {"dp": at[0] * n + there, "mp": mp}

    def x_device(step):
        return lax.rem(x + step + nx, nx) * CORES + core

    peers = [{"dp": dp, "mp": sibling}]
    if nx > 1:
        peers += [{"dp": dp, "mp": x_device(1)}, {"dp": dp, "mp": x_device(-1)}]
    for axis in (0, 1):
        peers += [along(axis, t) for t in range(1, n)]
    barrier = pltpu.get_barrier_semaphore()
    for peer in peers:
        pl.semaphore_signal(barrier, inc=1, device_id=peer, device_id_type=MESH)

    loads = [pltpu.make_async_copy(a, b, in_sem.at[i])
             for i, (a, b) in enumerate(((act_hbm, act), (docs_hbm, docs), (rb_hbm, rb), (grad_hbm, grad)))]
    for load in loads:
        load.start()
    loads[0].wait()
    for b in range(nb):
        feat[mp * nb + b] = act[:, b * BLOCK:(b + 1) * BLOCK].T
    pl.semaphore_wait(barrier, len(peers))

    def push(block, to, recv, send):
        return pltpu.make_async_remote_copy(
            src_ref=feat.at[block], dst_ref=feat.at[block], send_sem=send, recv_sem=recv,
            device_id={"dp": dp, "mp": to}, device_id_type=MESH)

    def share(block):
        push(block, sibling, sib_r.at[0], send_sem.at[1]).start()

    half = nb // 2
    if nx > 1:
        right, left, far = x_device(1), x_device(-1), x_device(2)

    def to_right(block, i):
        return push(block, right, x_r.at[0, i], send_sem.at[0])

    def to_left(block, i):
        return push(block, left, x_r.at[1, i], send_sem.at[0])

    turned = [*range(half, nb), *range(half)]
    if nx > 1:
        for b, e in zip(range(nb), turned):
            to_right(mp * nb + b, b).start()
            to_left(mp * nb + e, e).start()
    for b in range(nb):
        share(mp * nb + b)

    for load in loads[1:]:
        load.wait()
    live = docs[0, 0]
    for d in range(1, docs.shape[1]):
        live = live + docs[0, d]
    keep = lax.broadcasted_iota(jnp.int32, (slots, BLOCK), 0) < live
    for c in range(2 * per_half):
        tile = grad[:, c * BLOCK:(c + 1) * BLOCK]
        gm[c] = jnp.where(keep, tile, jnp.zeros_like(tile))

    if nx > 1:
        for b, e in zip(range(nb), turned):
            to_right(left * nb + b, b).wait_recv()
            if b < half:
                to_right(left * nb + b, nb + b).start()
            share(left * nb + b)
            to_left(right * nb + e, e).wait_recv()
            if e >= half:
                to_left(right * nb + e, half + e).start()
            share(right * nb + e)
        for b in range(half):
            to_right(far * nb + b, nb + b).wait_recv()
            share(far * nb + b)
            to_left(far * nb + half + b, nb + b).wait_recv()
            share(far * nb + half + b)
    everything = feat.at[pl.ds(0, nb * nx)]
    pltpu.make_async_remote_copy(
        src_ref=everything, dst_ref=everything, send_sem=send_sem.at[1], recv_sem=sib_r.at[0],
        device_id={"dp": dp, "mp": sibling}, device_id_type=MESH).wait_recv()

    def chunk(h, c, owner):
        if h == 0:
            return part[c, owner]
        wide = part[per_half + c, :, pl.ds(pl.multiple_of(owner * span, span), span), :]
        return wide.reshape(BLOCK, BLOCK)

    def hops(way, g):
        return steps if way == first_way(g) else n - 1 - steps

    plan, total = {}, 0
    for way in (0, 1):
        for g, (lo, hi) in enumerate(groups):
            for d in range(1, hops(way, g) + 1):
                for h in (0, 1):
                    plan[h, way, d, g] = (len(plan), total)
                    total += (hi - lo) * BLOCK + CODES

    def message(h, way, d, g):
        lo, hi = groups[g]
        index, first = plan[h, way, d, g]
        there = pl.ds(first, (hi - lo) * BLOCK + CODES)
        return pltpu.make_async_remote_copy(
            src_ref=sn.at[there], dst_ref=rn.at[there], send_sem=send_sem.at[2], recv_sem=m_r.at[index],
            device_id=along(h, 1 - 2 * way), device_id_type=MESH)

    def add_arrived(values, h, way, d, g):
        message(h, way, d, g).wait_recv()
        first = plan[h, way, d, g][1]
        last = first + len(values) * BLOCK
        scales = scales_of(rn[last:last + CODES, :])
        return [v + widen(rn[first + j * BLOCK:first + (j + 1) * BLOCK, :], scales[j:j + 1]) for j, v in enumerate(values)]

    def put(h, way, d, g, values):
        first = plan[h, way, d, g][1]
        last = first + len(values) * BLOCK
        codes = []
        for j, value in enumerate(values):
            q, code = quantize(value)
            sn[first + j * BLOCK:first + (j + 1) * BLOCK, :] = q
            codes.append(code)
        sn[last:last + CODES, :] = code_rows(codes)
        message(h, way, d, g).start()

    def products(h, g):
        for c in range(*groups[g]):
            column = h * per_half + c
            lhs = jnp.concatenate([feat[rb[column, k]] for k in range(knz)], axis=0)
            sums = jnp.dot(lhs, gm[column], preferred_element_type=jnp.float32)
            part[column] = sums.reshape(knz, BLOCK, BLOCK)

    def step(h, way, r, g):
        d = hops(way, g) - r
        if d < 1:
            return
        owner = lax.rem(at[h] + (1 - 2 * way) * d + n, n)
        values = [chunk(h, c, owner) for c in range(*groups[g])]
        if r > 0:
            values = add_arrived(values, h, way, d + 1, g)
        put(h, way, d, g, values)

    def second(h, t, g):
        lo, hi = groups[g]
        there = lax.rem(at[1 - h] + t, n)
        rows, scale_rows = pl.ds(lo * span, (hi - lo) * span), pl.ds(0, hi - lo)
        to = along(1 - h, t)
        data = pltpu.make_async_remote_copy(
            src_ref=s2.at[h, there, rows], dst_ref=r2.at[h, t, rows],
            send_sem=send_sem.at[3], recv_sem=m2_r.at[0, h, g], device_id=to, device_id_type=MESH)
        scale = pltpu.make_async_remote_copy(
            src_ref=c2.at[h, g, scale_rows], dst_ref=rc2.at[h, t, g, scale_rows],
            send_sem=send_sem.at[4], recv_sem=m2_r.at[1, h, g], device_id=to, device_id_type=MESH)
        return scale, data

    def own_step(h, g):
        lo, hi = groups[g]
        values = [chunk(h, c, at[h]) for c in range(lo, hi)]
        for way in (0, 1):
            if hops(way, g) > 0:
                values = add_arrived(values, h, way, 1, g)
        for j, value in enumerate(values):
            fin[h, lo + j] = value
            peak = jnp.maximum(jnp.max(jnp.abs(value), axis=0, keepdims=True), TINY)
            q = jnp.round(value * (TOP / peak)).astype(jnp.int32).astype(jnp.int16)
            for o in range(n):
                s2[h, o, (lo + j) * span:(lo + j + 1) * span, :] = q[o * span:(o + 1) * span]
            c2[h, g, j:j + 1, :] = peak * (1.0 / TOP)
        for t in sorted(range(1, n), key=lambda t: -min(t, n - t)):
            for copy in second(h, t, g):
                copy.start()

    def finish(h, g):
        lo, hi = groups[g]
        mine = pl.ds(pl.multiple_of(at[1 - h] * span, span), span)
        values = [fin[h, c, mine, :] for c in range(lo, hi)]
        if n > 1:
            others = pl.ds(1, n - 1)
            arrivals = (rc2.at[h, others, g, pl.ds(0, hi - lo)], r2.at[h, others, pl.ds(lo * span, (hi - lo) * span)])
            for i, ref in ((1, arrivals[0]), (0, arrivals[1])):
                pltpu.make_async_remote_copy(
                    src_ref=ref, dst_ref=ref, send_sem=send_sem.at[3 + i], recv_sem=m2_r.at[i, h, g],
                    device_id=along(1 - h, 1), device_id_type=MESH).wait_recv()
        for t in range(1, n):
            for j in range(hi - lo):
                rows = slice((lo + j) * span, (lo + j + 1) * span)
                values[j] = values[j] + widen(r2[h, t, rows, :], rc2[h, t, g, j:j + 1, :])
        for j in range(hi - lo):
            out[h * per_half + lo + j] = values[j] * factor

    order = [(h, g) for g in range(len(groups)) for h in (0, 1)]
    for r in range(max(1, steps)):
        for h, g in order:
            if r == 0:
                products(h, g)
            for way in (first_way(g), 1 - first_way(g)):
                step(h, way, r, g)
    for h, g in order:
        own_step(h, g)
    for h, g in order:
        finish(h, g)

    def sent(ref, i):
        pltpu.make_async_remote_copy(
            src_ref=ref, dst_ref=ref, send_sem=send_sem.at[i], recv_sem=sib_r.at[0],
            device_id={"dp": dp, "mp": sibling}, device_id_type=MESH).wait_send()

    if nx > 1:
        sent(feat.at[pl.ds(0, 3 * nb)], 0)
    sent(everything, 1)
    if n > 1:
        sent(sn, 2)
        sent(s2.at[:, pl.ds(1, n - 1)], 3)
        for g, (lo, hi) in enumerate(groups):
            sent(rc2.at[:, pl.ds(1, n - 1), g, pl.ds(0, hi - lo)], 4)


def shards(n, nx, groups, activations, out_grad, row_blocks, doc_lengths):
    slots = activations.shape[0]
    nb = activations.shape[1] // BLOCK
    columns, knz = row_blocks.shape
    per_half = columns // 2
    factor = 1.0 / math.sqrt(slots * n * n)
    cfg = (n, nx, nb, knz, per_half, groups, factor)
    ng = len(groups)
    span = BLOCK // n
    dma = pltpu.SemaphoreType.DMA
    anywhere = pl.BlockSpec(memory_space=pl.ANY)
    chains = [(hi - lo, n // 2 if way == first_way(g) else n - 1 - n // 2)
              for g, (lo, hi) in enumerate(groups) for way in (0, 1) for h in (0, 1)]
    messages = max(1, sum(hops for _, hops in chains))
    rows = max(CODES, sum(hops * (wide * BLOCK + CODES) for wide, hops in chains))
    return pl.pallas_call(
        functools.partial(kernel, cfg),
        out_shape=jax.ShapeDtypeStruct((columns, span * knz // n, BLOCK), jnp.float32),
        in_specs=[anywhere] * 4,
        out_specs=pl.BlockSpec(memory_space=pltpu.VMEM),
        scratch_shapes=[
            pltpu.VMEM(activations.shape, jnp.bfloat16),
            pltpu.VMEM(out_grad.shape, jnp.bfloat16),
            pltpu.SMEM(row_blocks.shape, jnp.int32),
            pltpu.SMEM(doc_lengths.shape, jnp.int32),
            pltpu.VMEM((nb * nx * CORES, BLOCK, slots), jnp.bfloat16),
            pltpu.VMEM((columns, slots, BLOCK), jnp.bfloat16),
            pltpu.VMEM((columns, knz, BLOCK, BLOCK), jnp.float32),
            pltpu.VMEM((rows, BLOCK), jnp.int16),
            pltpu.VMEM((rows, BLOCK), jnp.int16),
            pltpu.VMEM((2, n, per_half * span, BLOCK), jnp.int16),
            pltpu.VMEM((2, n, per_half * span, BLOCK), jnp.int16),
            pltpu.VMEM((2, ng, 8, BLOCK), jnp.float32),
            pltpu.VMEM((2, n, ng, 8, BLOCK), jnp.float32),
            pltpu.VMEM((2, per_half, BLOCK, BLOCK), jnp.float32),
            dma((4,)),
            dma((2, nb + nb // 2)),
            dma((1,)),
            dma((messages,)),
            dma((2, 2, ng)),
            dma((5,)),
        ],
        compiler_params=pltpu.CompilerParams(
            collective_id=0, has_side_effects=True, vmem_limit_bytes=56 * 2**20),
    )(activations, out_grad, row_blocks, doc_lengths)


def solution(mesh):
    n = math.isqrt(mesh.shape["dp"])
    body = functools.partial(shards, n, mesh.shape["mp"] // CORES, GROUPS)
    in_specs = (P("dp", "mp"), P("dp", "mp"), P("mp", None), P("dp", None))
    return jax.shard_map(body, mesh=mesh, in_specs=in_specs, out_specs=P("mp", "dp", None), check_vma=False)
```

time: 373 us -> 60.3 us (0.16)
  the two profiles are of different devices: /device:TPU:46 before, /device:TPU:1 now
where the time goes in v2:
time: 60.3 us; the launch traced here: 60.1 us
  Pallas kernels  57.2 us (95%)
  local copies, waits for them, and re-layouts  2.91 us (5%)
    pallas_call x1, Pallas kernels, shards(): pl.pallas_call(functools.partial(kernel, cfg), out_shape=jax.ShapeDtypeSt...  57.2 us
    unnamed x2, local copies, waits for them, and re-layouts  2.91 us

profile of v2, /device:TPU:1, one launch (start us, length us, event | category | flops | bytes accessed | tf_op | source)
XLA Modules:
  0.0 60.1 jit_solution(9585390819683521942)
XLA Ops:
  0.0 1.4 %copy.5.rb_hbm = s32[14,8]{1,0:T(8,128)} copy(s32[14,8]{0,1:T(8,128)} %param.6) | data formatting | bytes 896 | tf_op args[2]
  1.4 57.2 %shard_map.46 = f32[14,16,128]{2,1,0:T(8,128)} custom-call(bf16[256,512]{1,0:T(8,128)(2,1)} %act_hbm.1, bf16[256,1792]{1,0:T(8,128)(2,1)} %grad_hbm.1, s32[14,8]{1,0:T(8,128)} %copy.5.rb_hbm, s32[1,4]{1,0:T(1,128)} %docs_hbm.1), custom_call_target="tpu_custom_call" | custom-call | tf_op jit(solution)/shard_map/pallas_call | solution.py:290
  58.5 1.6 %copy.7 = f32[14,16,128]{2,1,0:T(8,128)} copy(f32[14,16,128]{2,1,0:T(8,128)} %shard_map.46) | data formatting | bytes 229376

commit v3 on v2

v3 whole, which is shorter than its diff:
```python
import functools
import math

import jax
import jax.numpy as jnp
from jax import lax
from jax.experimental import pallas as pl
from jax.experimental.pallas import tpu as pltpu
from jax.sharding import PartitionSpec as P

BLOCK = 128
CORES = 2
TOP = 32700.0
TINY = 1e-33
GROUPS = ((0, 1), (1, 2), (2, 3), (3, 5), (5, 7))
ORDER = (
    (0,), (1, 0, 3), (0, 0, 4), (1,), (1, 1, 4), (0, 1, 3), (2,), (3,), (1, 3, 4), (0, 2, 4), (4,), (0, 4, 4),
    (1, 2, 3), (1, 0, 2), (0, 0, 3), (1, 1, 3), (0, 3, 3), (1, 4, 3), (0, 2, 3), (1, 3, 3), (0, 1, 2), (0, 4, 3),
    (1, 2, 2), (1, 1, 2), (0, 0, 2), (1, 0, 1), (0, 3, 2), (1, 4, 2), (0, 1, 1), (1, 3, 2), (0, 2, 2), (0, 4, 2),
    (1, 1, 1), (1, 2, 1), (0, 0, 1), (0, 3, 1), (1, 4, 1), (0, 2, 1), (1, 3, 1), (1, 0), (0, 4, 1), (0, 0), (2, 0),
    (3, 0), (4, 0),
)
MESH = pl.DeviceIdType.MESH


def quantize(x):
    peak = jnp.maximum(jnp.max(jnp.abs(x), axis=0, keepdims=True), TINY)
    return jnp.round(x * (TOP / peak)).astype(jnp.int32).astype(jnp.int16), peak * (1.0 / TOP)


def widen(q, scale):
    return q.astype(jnp.int32).astype(jnp.float32) * scale


def hops_of(n, way, g):
    return n // 2 if way == g % 2 else n - 1 - n // 2


def order_of(n, groups):
    if n == 8 and groups == GROUPS:
        return ORDER
    order = []
    for r in range(max(1, n // 2)):
        for g in range(len(groups)):
            order += [(g,)] if r == 0 else []
            order += [(way, g, hops_of(n, way, g) - r) for way in (g % 2, 1 - g % 2) if hops_of(n, way, g) > r]
    return order + [(g, 0) for g in range(len(groups))]


def kernel(cfg, act_hbm, grad_hbm, rb_hbm, docs_hbm, out, act, grad, rb, docs, feat, gm, part, sn, rn, cn, rcn, s2, r2, c2, rc2, fin,
           in_sem, x_r, sib_r, m_r, m2_r, send_sem):
    n, nx, nb, knz, per_half, groups, factor = cfg
    slots = act.shape[0]
    span = BLOCK // n
    mid = BLOCK // 2
    dp = lax.axis_index("dp")
    mp = lax.axis_index("mp")
    at = (dp // n, lax.rem(dp, n))
    x, core = mp // CORES, lax.rem(mp, CORES)
    sibling = x * CORES + (1 - core)

    def along(axis, step):
        there = lax.rem(at[axis] + step + n, n)
        if axis == 0:
            return {"dp": there * n + at[1], "mp": mp}
        return {"dp": at[0] * n + there, "mp": mp}

    def x_device(step):
        return lax.rem(x + step + nx, nx) * CORES + core

    peers = [{"dp": dp, "mp": sibling}]
    if nx > 1:
        peers += [{"dp": dp, "mp": x_device(1)}, {"dp": dp, "mp": x_device(-1)}]
    for axis in (0, 1):
        peers += [along(axis, t) for t in range(1, n)]
    barrier = pltpu.get_barrier_semaphore()
    for peer in peers:
        pl.semaphore_signal(barrier, inc=1, device_id=peer, device_id_type=MESH)

    loads = [pltpu.make_async_copy(a, b, in_sem.at[i])
             for i, (a, b) in enumerate(((act_hbm, act), (docs_hbm, docs), (rb_hbm, rb), (grad_hbm, grad)))]
    for load in loads:
        load.start()
    loads[0].wait()
    for b in range(nb):
        feat[mp * nb + b] = act[:, b * BLOCK:(b + 1) * BLOCK].T
    pl.semaphore_wait(barrier, len(peers))

    def push(block, to, recv, send):
        return pltpu.make_async_remote_copy(
            src_ref=feat.at[block], dst_ref=feat.at[block], send_sem=send, recv_sem=recv,
            device_id={"dp": dp, "mp": to}, device_id_type=MESH)

    def share(block):
        push(block, sibling, sib_r.at[0], send_sem.at[1]).start()

    half = nb // 2
    if nx > 1:
        right, left, far = x_device(1), x_device(-1), x_device(2)

    def to_right(block, i):
        return push(block, right, x_r.at[0, i], send_sem.at[0])

    def to_left(block, i):
        return push(block, left, x_r.at[1, i], send_sem.at[0])

    turned = [*range(half, nb), *range(half)]
    if nx > 1:
        for b, e in zip(range(nb), turned):
            to_right(mp * nb + b, b).start()
            to_left(mp * nb + e, e).start()
    for b in range(nb):
        share(mp * nb + b)

    for load in loads[1:]:
        load.wait()
    live = docs[0, 0]
    for d in range(1, docs.shape[1]):
        live = live + docs[0, d]
    keep = lax.broadcasted_iota(jnp.int32, (slots, BLOCK), 0) < live
    for c in range(2 * per_half):
        tile = grad[:, c * BLOCK:(c + 1) * BLOCK]
        gm[c] = jnp.where(keep, tile, jnp.zeros_like(tile))

    if nx > 1:
        for b, e in zip(range(nb), turned):
            to_right(left * nb + b, b).wait_recv()
            if b < half:
                to_right(left * nb + b, nb + b).start()
            share(left * nb + b)
            to_left(right * nb + e, e).wait_recv()
            if e >= half:
                to_left(right * nb + e, half + e).start()
            share(right * nb + e)
        for b in range(half):
            to_right(far * nb + b, nb + b).wait_recv()
            share(far * nb + b)
            to_left(far * nb + half + b, nb + b).wait_recv()
            share(far * nb + half + b)
    everything = feat.at[pl.ds(0, nb * nx)]
    pltpu.make_async_remote_copy(
        src_ref=everything, dst_ref=everything, send_sem=send_sem.at[1], recv_sem=sib_r.at[0],
        device_id={"dp": dp, "mp": sibling}, device_id_type=MESH).wait_recv()

    def chunk(h, c, owner):
        if h == 0:
            return part[c, owner]
        wide = part[per_half + c, :, pl.ds(pl.multiple_of(owner * span, span), span), :]
        return wide.reshape(BLOCK, BLOCK)

    plan, count = {}, 0
    for way in (0, 1):
        for g, (lo, hi) in enumerate(groups):
            for d in range(1, hops_of(n, way, g) + 1):
                for h in (0, 1):
                    plan[h, way, d, g] = (len(plan), count)
                    count += hi - lo

    def remote(src, dst, send, recv, to):
        return pltpu.make_async_remote_copy(
            src_ref=src, dst_ref=dst, send_sem=send_sem.at[send], recv_sem=recv, device_id=to, device_id_type=MESH)

    def message(h, way, d, g):
        lo, hi = groups[g]
        index, first = plan[h, way, d, g]
        to = along(h, 1 - 2 * way)
        rows, scales = pl.ds(first * BLOCK, (hi - lo) * BLOCK), pl.ds(first, hi - lo)
        return (remote(cn.at[scales], rcn.at[scales], 4, m_r.at[index], to),
                remote(sn.at[rows], rn.at[rows], 2, m_r.at[index], to))

    def add_arrived(values, h, way, d, g):
        index, first = plan[h, way, d, g]
        both = part.at[pl.ds(0, len(values)), 0, pl.ds(0, mid + 1)]
        remote(both, both, 2, m_r.at[index], along(h, 1 - 2 * way)).wait_recv()
        return [v + widen(rn[(first + j) * BLOCK:(first + j + 1) * BLOCK, :], rcn[first + j:first + j + 1, :])
                for j, v in enumerate(values)]

    def put(h, way, d, g, values):
        first = plan[h, way, d, g][1]
        for j, value in enumerate(values):
            q, scale = quantize(value)
            sn[(first + j) * BLOCK:(first + j + 1) * BLOCK, :] = q
            cn[first + j:first + j + 1, :] = scale
        for copy in message(h, way, d, g):
            copy.start()

    def products(h, g):
        for c in range(*groups[g]):
            column = h * per_half + c
            lhs = jnp.concatenate([feat[rb[k, column]] for k in range(knz)], axis=0)
            sums = jnp.dot(lhs, gm[column], preferred_element_type=jnp.float32)
            part[column] = sums.reshape(knz, BLOCK, BLOCK)

    def step(h, way, g, d):
        owner = lax.rem(at[h] + (1 - 2 * way) * d + n, n)
        values = [chunk(h, c, owner) for c in range(*groups[g])]
        if d < hops_of(n, way, g):
            values = add_arrived(values, h, way, d + 1, g)
        put(h, way, d, g, values)

    def second(h, t, g):
        lo, hi = groups[g]
        there = lax.rem(at[1 - h] + t, n)
        rows, scales = pl.ds(lo * span, (hi - lo) * span), pl.ds(lo, hi - lo)
        to = along(1 - h, t)
        return (remote(c2.at[h, scales], rc2.at[h, t, scales], 5, m2_r.at[h, g], to),
                remote(s2.at[h, there, rows], r2.at[h, t, rows], 3, m2_r.at[h, g], to))

    def own_step(h, g):
        lo, hi = groups[g]
        values = [chunk(h, c, at[h]) for c in range(lo, hi)]
        for way in (0, 1):
            if hops_of(n, way, g) > 0:
                values = add_arrived(values, h, way, 1, g)
        for j, value in enumerate(values):
            fin[h, lo + j] = value
            q, scale = quantize(value)
            for o in range(n):
                s2[h, o, (lo + j) * span:(lo + j + 1) * span, :] = q[o * span:(o + 1) * span]
            c2[h, lo + j:lo + j + 1, :] = scale
        for t in sorted(range(1, n), key=lambda t: -min(t, n - t)):
            for copy in second(h, t, g):
                copy.start()

    def finish(h, g):
        lo, hi = groups[g]
        mine = pl.ds(pl.multiple_of(at[1 - h] * span, span), span)
        values = [fin[h, c, mine, :] for c in range(lo, hi)]
        if n > 1:
            both = part.at[pl.ds(0, n - 1), 0, pl.ds(0, (hi - lo) * (span // 2 + 1))]
            remote(both, both, 3, m2_r.at[h, g], along(1 - h, 1)).wait_recv()
        for t in range(1, n):
            for j in range(hi - lo):
                rows = slice((lo + j) * span, (lo + j + 1) * span)
                values[j] = values[j] + widen(r2[h, t, rows, :], rc2[h, t, lo + j:lo + j + 1, :])
        for j in range(hi - lo):
            out[h * per_half + lo + j] = values[j] * factor

    finishing = []
    for op in order_of(n, groups):
        for h in (0, 1):
            if len(op) == 1:
                products(h, *op)
            elif len(op) == 3:
                step(h, *op)
            else:
                own_step(h, op[0])
                finishing.append((h, op[0]))
    for h, g in finishing:
        finish(h, g)

    def sent(ref, i):
        pltpu.make_async_remote_copy(
            src_ref=ref, dst_ref=ref, send_sem=send_sem.at[i], recv_sem=sib_r.at[0],
            device_id={"dp": dp, "mp": sibling}, device_id_type=MESH).wait_send()

    if nx > 1:
        sent(feat.at[pl.ds(0, 3 * nb)], 0)
    sent(everything, 1)
    if n > 1:
        sent(sn, 2)
        sent(cn, 4)
        sent(s2.at[:, pl.ds(1, n - 1)], 3)
        sent(rc2.at[:, pl.ds(1, n - 1), pl.ds(0, per_half)], 5)


def shards(n, nx, groups, activations, out_grad, row_blocks, doc_lengths):
    slots = activations.shape[0]
    nb = activations.shape[1] // BLOCK
    columns, knz = row_blocks.shape
    per_half = columns // 2
    factor = 1.0 / math.sqrt(slots * n * n)
    cfg = (n, nx, nb, knz, per_half, groups, factor)
    ng = len(groups)
    span = BLOCK // n
    dma = pltpu.SemaphoreType.DMA
    anywhere = pl.BlockSpec(memory_space=pl.ANY)
    chains = [(hi - lo, hops_of(n, way, g)) for g, (lo, hi) in enumerate(groups) for way in (0, 1) for h in (0, 1)]
    messages = max(1, sum(hops for _, hops in chains))
    blocks = max(1, sum(hops * wide for wide, hops in chains))
    return pl.pallas_call(
        functools.partial(kernel, cfg),
        out_shape=jax.ShapeDtypeStruct((columns, span * knz // n, BLOCK), jnp.float32),
        in_specs=[anywhere] * 4,
        out_specs=pl.BlockSpec(memory_space=pltpu.VMEM),
        scratch_shapes=[
            pltpu.VMEM(activations.shape, jnp.bfloat16),
            pltpu.VMEM(out_grad.shape, jnp.bfloat16),
            pltpu.SMEM(row_blocks.shape[::-1], jnp.int32),
            pltpu.SMEM(doc_lengths.shape, jnp.int32),
            pltpu.VMEM((nb * nx * CORES, BLOCK, slots), jnp.bfloat16),
            pltpu.VMEM((columns, slots, BLOCK), jnp.bfloat16),
            pltpu.VMEM((columns, knz, BLOCK, BLOCK), jnp.float32),
            pltpu.VMEM((blocks * BLOCK, BLOCK), jnp.int16),
            pltpu.VMEM((blocks * BLOCK, BLOCK), jnp.int16),
            pltpu.VMEM((blocks, BLOCK), jnp.float32),
            pltpu.VMEM((blocks, BLOCK), jnp.float32),
            pltpu.VMEM((2, n, per_half * span, BLOCK), jnp.int16),
            pltpu.VMEM((2, n, per_half * span, BLOCK), jnp.int16),
            pltpu.VMEM((2, 8, BLOCK), jnp.float32),
            pltpu.VMEM((2, n, 8, BLOCK), jnp.float32),
            pltpu.VMEM((2, per_half, BLOCK, BLOCK), jnp.float32),
            dma((4,)),
            dma((2, nb + nb // 2)),
            dma((1,)),
            dma((messages,)),
            dma((2, ng)),
            dma((6,)),
        ],
        compiler_params=pltpu.CompilerParams(
            collective_id=0, has_side_effects=True, vmem_limit_bytes=40 * 2**20),
    )(*(pltpu.with_memory_space_constraint(a, pltpu.HBM) for a in (activations, out_grad, row_blocks.T, doc_lengths)))


def solution(mesh):
    n = math.isqrt(mesh.shape["dp"])
    body = functools.partial(shards, n, mesh.shape["mp"] // CORES, GROUPS)
    in_specs = (P("dp", "mp"), P("dp", "mp"), P("mp", None), P("dp", None))
    return jax.shard_map(body, mesh=mesh, in_specs=in_specs, out_specs=P("mp", "dp", None), check_vma=False)
```

time: 60.3 us -> 56.1 us (0.930)
  local copies, waits for them, and re-layouts: 2.91 us -> 0.65 us
  Pallas kernels: 57.2 us -> 55.3 us
    unnamed x2 -> x1, local copies, waits for them, and re-layouts: 2.91 us -> 0.65 us
    pallas_call x1, Pallas kernels: 57.2 us -> 55.3 us  [shards(): pl.pallas_call(functools.partial(kernel, cfg), out_shape=jax.ShapeDtypeSt...]
where the time goes in v3:
time: 56.1 us; the launch traced here: 56 us
  Pallas kernels  55.3 us (99%)
  local copies, waits for them, and re-layouts  0.65 us (1%)
    pallas_call x1, Pallas kernels, shards(): pl.pallas_call(functools.partial(kernel, cfg), out_shape=jax.ShapeDtypeSt...  55.3 us

profile of v3, /device:TPU:1, one launch (start us, length us, event | category | flops | bytes accessed | tf_op | source)
XLA Modules:
  0.0 56.0 jit_solution(7754458775214312274)
XLA Ops:
  0.0 55.3 %shard_map.46 = f32[14,16,128]{2,1,0:T(8,128)S(1)} custom-call(bf16[256,512]{1,0:T(8,128)(2,1)} %act_hbm.1, bf16[256,1792]{1,0:T(8,128)(2,1)} %grad_hbm.1, s32[8,14]{1,0:T(8,128)} %bitcast.1, s32[1,4]{1,0:T(1,128)} %docs_hbm.1), custom_call_target="tpu_custom_call" | custom-call | tf_op jit(solution)/shard_map/pallas_call | solution.py:281
  55.4 0.6 %copy.6 = f32[14,16,128]{2,1,0:T(8,128)} copy(f32[14,16,128]{2,1,0:T(8,128)S(1)} %shard_map.46) | data formatting | bytes 229376

commit v4 on v0

v4 whole, which is shorter than its diff:
```python
import functools
import math

import jax
import jax.numpy as jnp
from jax import lax
from jax.experimental import pallas as pl
from jax.experimental.pallas import tpu as pltpu
from jax.sharding import PartitionSpec as P

BLOCK = 128
CORES = 2
TOP = 32700.0
TINY = 1e-33
LEAD = 3
ORDER = (
    ("near", 0), ("near", 1), ("near", 2), ("far", 0), ("near", 3), ("unit", 0), ("far", 1), ("sum", 0, 0, 0, 4),
    ("sum", 1, 0, 0, 4), ("near", 4), ("sum", 1, 1, 1, 4), ("far", 2), ("sum", 0, 1, 0, 3), ("sum", 1, 0, 2, 4),
    ("unit", 1), ("near", 5), ("unit", 2), ("far", 3), ("sum", 0, 1, 1, 4), ("sum", 1, 0, 1, 3), ("sum", 0, 0, 1, 3),
    ("near", 6), ("sum", 1, 1, 0, 3), ("unit", 3), ("far", 4), ("sum", 0, 0, 0, 3), ("near", 7), ("sum", 0, 1, 0, 2),
    ("sum", 1, 1, 3, 4), ("sum", 1, 0, 0, 3), ("far", 5), ("unit", 4), ("sum", 0, 0, 2, 4), ("unit", 5), ("far", 6),
    ("sum", 1, 1, 1, 3), ("sum", 1, 0, 2, 3), ("sum", 0, 1, 1, 3), ("sum", 0, 0, 1, 2), ("far", 7), ("unit", 6),
    ("sum", 0, 1, 3, 4), ("sum", 0, 0, 0, 2), ("unit", 7), ("sum", 1, 0, 0, 2), ("sum", 0, 1, 2, 3),
    ("sum", 1, 0, 1, 2), ("sum", 1, 1, 0, 2), ("sum", 0, 0, 4, 4), ("sum", 1, 1, 4, 3), ("sum", 0, 0, 2, 3),
    ("sum", 0, 1, 4, 3), ("sum", 1, 1, 2, 3), ("sum", 1, 0, 4, 4), ("sum", 0, 1, 0, 1), ("sum", 1, 0, 2, 2),
    ("sum", 0, 0, 3, 3), ("sum", 0, 1, 1, 2), ("sum", 1, 1, 1, 2), ("sum", 1, 0, 3, 3), ("sum", 0, 0, 0, 1),
    ("sum", 0, 1, 3, 3), ("sum", 1, 1, 3, 3), ("sum", 0, 0, 1, 1), ("sum", 1, 0, 0, 1), ("sum", 0, 1, 2, 2),
    ("sum", 1, 0, 1, 1), ("sum", 0, 0, 2, 2), ("sum", 1, 1, 0, 1), ("sum", 1, 1, 2, 2), ("sum", 0, 1, 4, 2),
    ("sum", 1, 0, 4, 3), ("sum", 0, 0, 4, 3), ("sum", 0, 1, 1, 1), ("sum", 1, 1, 1, 1), ("own", 0, 0),
    ("sum", 0, 0, 3, 2), ("sum", 0, 1, 3, 2), ("sum", 1, 1, 3, 2), ("sum", 1, 0, 3, 2), ("own", 1, 0),
    ("sum", 1, 0, 2, 1), ("sum", 0, 0, 2, 1), ("sum", 1, 1, 4, 2), ("sum", 1, 1, 2, 1), ("sum", 0, 1, 2, 1),
    ("sum", 0, 0, 4, 2), ("sum", 1, 0, 4, 2), ("own", 0, 1), ("own", 1, 1), ("sum", 0, 0, 3, 1), ("sum", 1, 0, 3, 1),
    ("sum", 1, 1, 3, 1), ("sum", 0, 1, 3, 1), ("sum", 1, 1, 4, 1), ("sum", 0, 1, 4, 1), ("sum", 0, 0, 4, 1),
    ("sum", 1, 0, 4, 1), ("own", 1, 2), ("own", 0, 2), ("own", 1, 3), ("own", 0, 3), ("own", 1, 4), ("own", 0, 4),
)
MESH = pl.DeviceIdType.MESH


def quantize(x):
    peak = jnp.maximum(jnp.max(jnp.abs(x), axis=0, keepdims=True), TINY)
    return jnp.round(x * (TOP / peak)).astype(jnp.int32).astype(jnp.int16), peak * (1.0 / TOP)


def widen(q, scale):
    return q.astype(jnp.int32).astype(jnp.float32) * scale


def offsets_of(n):
    return sorted(range(n), key=lambda o: (-min(o, n - o), o))


def groups_of(n):
    return [[o for o in offsets_of(n) if min(o, n - o) == d] for d in range(n // 2, -1, -1)]


def hops_of(n, way, g):
    return n // 2 if way == g % 2 else n - 1 - n // 2


def order_of(n):
    if n == 8:
        return ORDER
    order = []
    for j in range(n):
        order += [("near", j), ("far", j), ("unit", j)]
    groups = range(len(groups_of(n)))
    for r in range(n // 2):
        for g in groups:
            for h in (0, 1):
                order += [("sum", h, way, g, hops_of(n, way, g) - r)
                          for way in (g % 2, 1 - g % 2) if hops_of(n, way, g) > r]
    return order + [("own", h, g) for g in groups for h in (0, 1)]


def kernel(cfg, act_hbm, grad_hbm, rb_hbm, docs_hbm, out, act, grad, rb, docs, turn, gm, unit, gauge, sn, rn, cn, rcn,
           s2, r2, c2, rc2, in_sem, x_r, sib_r, m_r, m2_r, send_sem, *feats):
    n, nx, nb, knz, per_half, factor = cfg
    slots = act.shape[0]
    span = BLOCK // n
    high = per_half * span
    offsets, groups = offsets_of(n), groups_of(n)
    place = {o: j for j, o in enumerate(offsets)}
    dp = lax.axis_index("dp")
    mp = lax.axis_index("mp")
    at = (dp // n, lax.rem(dp, n))
    x, core = mp // CORES, lax.rem(mp, CORES)
    sibling = x * CORES + (1 - core)

    def along(axis, step):
        there = lax.rem(at[axis] + step + n, n)
        if axis == 0:
            return {"dp": there * n + at[1], "mp": mp}
        return {"dp": at[0] * n + there, "mp": mp}

    def x_device(step):
        return lax.rem(x + step + nx, nx) * CORES + core

    peers = [{"dp": dp, "mp": sibling}]
    if nx > 1:
        peers += [{"dp": dp, "mp": x_device(1)}, {"dp": dp, "mp": x_device(-1)}]
    if n > 1:
        peers += [along(axis, step) for axis in (0, 1) for step in sorted({1, n - 1, 2 % n, (n - 2) % n} - {0})]
    barrier = pltpu.get_barrier_semaphore()
    for peer in peers:
        pl.semaphore_signal(barrier, inc=1, device_id=peer, device_id_type=MESH)

    loads = [pltpu.make_async_copy(a, b, in_sem.at[i])
             for i, (a, b) in enumerate(((act_hbm, act), (docs_hbm, docs), (rb_hbm, rb), (grad_hbm, grad)))]
    for load in loads:
        load.start()
    loads[0].wait()
    for b in range(nb):
        turn[b] = act[:, b * BLOCK:(b + 1) * BLOCK].T

    def cut(j):
        rows = pl.ds(pl.multiple_of(lax.rem(at[1] + offsets[j], n) * span, span), span)
        for b in range(nb):
            feats[j][mp * nb + b] = turn[b, rows, :]

    for j in range(n):
        cut(j)
    pl.semaphore_wait(barrier, len(peers))

    def remote(src, dst, send, recv, to):
        return pltpu.make_async_remote_copy(
            src_ref=src, dst_ref=dst, send_sem=send_sem.at[send], recv_sem=recv, device_id=to, device_id_type=MESH)

    def push(j, first, size, to, send, recv):
        piece = feats[j].at[pl.ds(first, size)]
        return remote(piece, piece, send, recv, {"dp": dp, "mp": to})

    def share(j, first, size):
        push(j, first, size, sibling, 1, sib_r.at[j]).start()

    half = nb // 2
    if nx > 1:
        right, left, far = x_device(1), x_device(-1), x_device(2)

    def give(j):
        if nx > 1:
            push(j, mp * nb, nb, right, 0, x_r.at[0, j]).start()
            push(j, mp * nb, nb, left, 0, x_r.at[1, j]).start()
        share(j, mp * nb, nb)

    for j in range(min(LEAD, n)):
        give(j)

    for load in loads[1:]:
        load.wait()
    live = docs[0, 0]
    for d in range(1, docs.shape[1]):
        live = live + docs[0, d]
    keep = lax.broadcasted_iota(jnp.int32, (slots, BLOCK), 0) < live
    for c in range(2 * per_half):
        tile = grad[:, c * BLOCK:(c + 1) * BLOCK]
        gm[c] = jnp.where(keep, tile, jnp.zeros_like(tile))

    def near(j):
        if nx > 1:
            push(j, left * nb, nb, right, 0, x_r.at[0, j]).wait_recv()
            push(j, left * nb, half, right, 0, x_r.at[2, j]).start()
            push(j, right * nb, nb, left, 0, x_r.at[1, j]).wait_recv()
            push(j, right * nb + half, half, left, 0, x_r.at[3, j]).start()
        if j + LEAD < n:
            give(j + LEAD)
        if nx > 1:
            share(j, left * nb, nb)
            share(j, right * nb, nb)

    def from_far(j):
        if nx > 1:
            push(j, far * nb, half, right, 0, x_r.at[2, j]).wait_recv()
            share(j, far * nb, half)
            push(j, far * nb + half, half, left, 0, x_r.at[3, j]).wait_recv()
            share(j, far * nb + half, half)

    def products(j):
        push(j, 0, nb * nx, sibling, 1, sib_r.at[j]).wait_recv()
        for c in range(2 * per_half):
            lhs = jnp.concatenate([feats[j][rb[k, c]] for k in range(knz)], axis=0)
            sums = jnp.dot(lhs, gm[c], preferred_element_type=jnp.float32)
            unit[j, :, c] = sums.reshape(knz, span, BLOCK)

    def chunk(h, step, o):
        to_y, to_z = (step, o) if h == 0 else (o, step)
        k = lax.rem(at[0] + to_y + n, n)
        return unit[place[to_z % n], k, h * per_half:(h + 1) * per_half].reshape(high, BLOCK)

    plan, count = {}, 0
    for way in (0, 1):
        for g, group in enumerate(groups):
            for d in range(1, hops_of(n, way, g) + 1):
                for h in (0, 1):
                    plan[h, way, d, g] = (len(plan), count)
                    count += len(group)

    def message(h, way, d, g):
        index, first = plan[h, way, d, g]
        size = len(groups[g])
        to = along(h, 1 - 2 * way)
        rows, scales = pl.ds(first * high, size * high), pl.ds(first, size)
        return (remote(cn.at[scales], rcn.at[scales], 4, m_r.at[index], to),
                remote(sn.at[rows], rn.at[rows], 2, m_r.at[index], to))

    def add_arrived(values, h, way, d, g):
        index, first = plan[h, way, d, g]
        both = gauge.at[pl.ds(0, len(values))]
        remote(both, both, 2, m_r.at[index], along(h, 1 - 2 * way)).wait_recv()
        return [v + widen(rn[(first + i) * high:(first + i + 1) * high, :], rcn[first + i:first + i + 1, :])
                for i, v in enumerate(values)]

    def step(h, way, g, d):
        values = [chunk(h, (1 - 2 * way) * d, o) for o in groups[g]]
        if d < hops_of(n, way, g):
            values = add_arrived(values, h, way, d + 1, g)
        first = plan[h, way, d, g][1]
        for i, value in enumerate(values):
            q, scale = quantize(value)
            sn[(first + i) * high:(first + i + 1) * high, :] = q
            cn[first + i:first + i + 1, :] = scale
        for copy in message(h, way, d, g):
            copy.start()

    def way_of(h, o):
        return 0 if o < n - o or (o == n - o and h == 0) else 1

    def target(h, o):
        hop = min(2, o, n - o)
        return ((o - hop) % n, hop) if way_of(h, o) == 0 else ((o + hop) % n, -hop)

    def second(h, o):
        to = along(1 - h, target(h, o)[1])
        row = pl.ds(h * n + o, 1)
        return (remote(c2.at[row], rc2.at[row], 5, m2_r.at[h, o], to),
                remote(s2.at[h, o], r2.at[h, o], 3, m2_r.at[h, o], to))

    def add_second(value, h, o):
        both = gauge.at[pl.ds(0, 1)]
        remote(both, both, 3, m2_r.at[h, o], along(1 - h, 1)).wait_recv()
        return value + widen(r2[h, o], rc2[h * n + o:h * n + o + 1, :])

    def own_step(h, g):
        values = [chunk(h, 0, o) for o in groups[g]]
        for way in (0, 1):
            if hops_of(n, way, g) > 0:
                values = add_arrived(values, h, way, 1, g)
        for value, o in zip(values, groups[g]):
            for before in range(1, n):
                if target(h, before)[0] == o:
                    value = add_second(value, h, before)
            if o == 0:
                out[h * per_half:(h + 1) * per_half] = (value * factor).reshape(per_half, span, BLOCK)
            else:
                q, scale = quantize(value)
                s2[h, o] = q
                c2[h * n + o:h * n + o + 1, :] = scale
                for copy in second(h, o):
                    copy.start()

    run = {"near": near, "far": from_far, "unit": products, "sum": step, "own": own_step}
    for op in order_of(n):
        run[op[0]](*op[1:])

    def sent(ref, i):
        remote(ref, ref, i, sib_r.at[0], {"dp": dp, "mp": sibling}).wait_send()

    for j in range(n):
        if nx > 1:
            sent(feats[j].at[pl.ds(0, 3 * nb)], 0)
        sent(feats[j].at[pl.ds(0, nb * nx)], 1)
    if n > 1:
        sent(sn, 2)
        sent(cn, 4)
        sent(s2.at[:, pl.ds(1, n - 1)], 3)
        sent(rc2.at[pl.ds(0, 2 * (n - 1))], 5)


def shards(n, nx, activations, out_grad, row_blocks, doc_lengths):
    slots = activations.shape[0]
    nb = activations.shape[1] // BLOCK
    columns, knz = row_blocks.shape
    per_half = columns // 2
    factor = 1.0 / math.sqrt(slots * n * n)
    span = BLOCK // n
    high = per_half * span
    sizes = [(len(group), hops_of(n, way, g)) for g, group in enumerate(groups_of(n)) for way in (0, 1) for h in (0, 1)]
    messages = max(1, sum(hops for _, hops in sizes))
    count = max(1, sum(hops * size for size, hops in sizes))
    dma = pltpu.SemaphoreType.DMA
    operands = (activations, out_grad, row_blocks.T, doc_lengths)
    return pl.pallas_call(
        functools.partial(kernel, (n, nx, nb, knz, per_half, factor)),
        out_shape=jax.ShapeDtypeStruct((columns, span * knz // n, BLOCK), jnp.float32),
        in_specs=[pl.BlockSpec(memory_space=pl.ANY)] * 4,
        out_specs=pl.BlockSpec(memory_space=pltpu.VMEM),
        scratch_shapes=[
            pltpu.VMEM(activations.shape, jnp.bfloat16),
            pltpu.VMEM(out_grad.shape, jnp.bfloat16),
            pltpu.SMEM(row_blocks.shape[::-1], jnp.int32),
            pltpu.SMEM(doc_lengths.shape, jnp.int32),
            pltpu.VMEM((nb, BLOCK, slots), jnp.bfloat16),
            pltpu.VMEM((columns, slots, BLOCK), jnp.bfloat16),
            pltpu.VMEM((n, knz, columns, span, BLOCK), jnp.float32),
            pltpu.VMEM((2, high // 2 + 1, BLOCK), jnp.float32),
            pltpu.VMEM((count * high, BLOCK), jnp.int16),
            pltpu.VMEM((count * high, BLOCK), jnp.int16),
            pltpu.VMEM((count, BLOCK), jnp.float32),
            pltpu.VMEM((count, BLOCK), jnp.float32),
            pltpu.VMEM((2, n, high, BLOCK), jnp.int16),
            pltpu.VMEM((2, n, high, BLOCK), jnp.int16),
            pltpu.VMEM((2 * n, BLOCK), jnp.float32),
            pltpu.VMEM((2 * n, BLOCK), jnp.float32),
            dma((4,)),
            dma((4, n)),
            dma((n,)),
            dma((messages,)),
            dma((2, n)),
            dma((6,)),
        ] + [pltpu.VMEM((nb * nx * CORES, span, slots), jnp.bfloat16)] * n,
        compiler_params=pltpu.CompilerParams(
            collective_id=0, has_side_effects=True, vmem_limit_bytes=40 * 2**20),
    )(*(pltpu.with_memory_space_constraint(a, pltpu.HBM) for a in operands))


def solution(mesh):
    n = math.isqrt(mesh.shape["dp"])
    body = functools.partial(shards, n, mesh.shape["mp"] // CORES)
    in_specs = (P("dp", "mp"), P("dp", "mp"), P("mp", None), P("dp", None))
    return jax.shard_map(body, mesh=mesh, in_specs=in_specs, out_specs=P("mp", "dp", None), check_vma=False)
```

time: 373 us -> 53.5 us (0.14)
  the two profiles are of different devices: /device:TPU:46 before, /device:TPU:8 now
where the time goes in v4:
time: 53.5 us; the launch traced here: 53.4 us
  Pallas kernels  52.7 us (99%)
  local copies, waits for them, and re-layouts  0.65 us (1%)
    pallas_call x1, Pallas kernels, shards(): pl.pallas_call(functools.partial(kernel, (n, nx, nb, knz, per_half, facto...  52.7 us

profile of v4, /device:TPU:8, one launch (start us, length us, event | category | flops | bytes accessed | tf_op | source)
XLA Modules:
  0.0 53.4 jit_solution(4151319526523408683)
XLA Ops:
  0.0 52.7 %shard_map.46 = f32[14,16,128]{2,1,0:T(8,128)S(1)} custom-call(bf16[256,512]{1,0:T(8,128)(2,1)} %act_hbm.1, bf16[256,1792]{1,0:T(8,128)(2,1)} %grad_hbm.1, s32[8,14]{1,0:T(8,128)} %bitcast.1, s32[1,4]{1,0:T(1,128)} %docs_hbm.1), custom_call_target="tpu_custom_call" | custom-call | tf_op jit(solution)/shard_map/pallas_call | solution.py:291
  52.7 0.6 %copy.6 = f32[14,16,128]{2,1,0:T(8,128)} copy(f32[14,16,128]{2,1,0:T(8,128)S(1)} %shard_map.46) | data formatting | bytes 229376

commit v5 on v4

--- a/solution.py
+++ b/solution.py
@@ -13,27 +13,32 @@
 TOP = 32700.0
 TINY = 1e-33
 LEAD = 3
+DIRECT = 4
+FIRST = 6
+MESH = pl.DeviceIdType.MESH
 ORDER = (
-    ("near", 0), ("near", 1), ("near", 2), ("far", 0), ("near", 3), ("unit", 0), ("far", 1), ("sum", 0, 0, 0, 4),
-    ("sum", 1, 0, 0, 4), ("near", 4), ("sum", 1, 1, 1, 4), ("far", 2), ("sum", 0, 1, 0, 3), ("sum", 1, 0, 2, 4),
-    ("unit", 1), ("near", 5), ("unit", 2), ("far", 3), ("sum", 0, 1, 1, 4), ("sum", 1, 0, 1, 3), ("sum", 0, 0, 1, 3),
-    ("near", 6), ("sum", 1, 1, 0, 3), ("unit", 3), ("far", 4), ("sum", 0, 0, 0, 3), ("near", 7), ("sum", 0, 1, 0, 2),
-    ("sum", 1, 1, 3, 4), ("sum", 1, 0, 0, 3), ("far", 5), ("unit", 4), ("sum", 0, 0, 2, 4), ("unit", 5), ("far", 6),
-    ("sum", 1, 1, 1, 3), ("sum", 1, 0, 2, 3), ("sum", 0, 1, 1, 3), ("sum", 0, 0, 1, 2), ("far", 7), ("unit", 6),
-    ("sum", 0, 1, 3, 4), ("sum", 0, 0, 0, 2), ("unit", 7), ("sum", 1, 0, 0, 2), ("sum", 0, 1, 2, 3),
-    ("sum", 1, 0, 1, 2), ("sum", 1, 1, 0, 2), ("sum", 0, 0, 4, 4), ("sum", 1, 1, 4, 3), ("sum", 0, 0, 2, 3),
-    ("sum", 0, 1, 4, 3), ("sum", 1, 1, 2, 3), ("sum", 1, 0, 4, 4), ("sum", 0, 1, 0, 1), ("sum", 1, 0, 2, 2),
-    ("sum", 0, 0, 3, 3), ("sum", 0, 1, 1, 2), ("sum", 1, 1, 1, 2), ("sum", 1, 0, 3, 3), ("sum", 0, 0, 0, 1),
-    ("sum", 0, 1, 3, 3), ("sum", 1, 1, 3, 3), ("sum", 0, 0, 1, 1), ("sum", 1, 0, 0, 1), ("sum", 0, 1, 2, 2),
-    ("sum", 1, 0, 1, 1), ("sum", 0, 0, 2, 2), ("sum", 1, 1, 0, 1), ("sum", 1, 1, 2, 2), ("sum", 0, 1, 4, 2),
-    ("sum", 1, 0, 4, 3), ("sum", 0, 0, 4, 3), ("sum", 0, 1, 1, 1), ("sum", 1, 1, 1, 1), ("own", 0, 0),
-    ("sum", 0, 0, 3, 2), ("sum", 0, 1, 3, 2), ("sum", 1, 1, 3, 2), ("sum", 1, 0, 3, 2), ("own", 1, 0),
-    ("sum", 1, 0, 2, 1), ("sum", 0, 0, 2, 1), ("sum", 1, 1, 4, 2), ("sum", 1, 1, 2, 1), ("sum", 0, 1, 2, 1),
-    ("sum", 0, 0, 4, 2), ("sum", 1, 0, 4, 2), ("own", 0, 1), ("own", 1, 1), ("sum", 0, 0, 3, 1), ("sum", 1, 0, 3, 1),
-    ("sum", 1, 1, 3, 1), ("sum", 0, 1, 3, 1), ("sum", 1, 1, 4, 1), ("sum", 0, 1, 4, 1), ("sum", 0, 0, 4, 1),
-    ("sum", 1, 0, 4, 1), ("own", 1, 2), ("own", 0, 2), ("own", 1, 3), ("own", 0, 3), ("own", 1, 4), ("own", 0, 4),
+    ("near", 0), ("far", 0), ("near", 1), ("unit", 0, 1), ("unit", 0, 0), ("near", 2), ("far", 1),
+    ("sum", 1, 0, 0, 4), ("sum", 1, 0, 4, 4), ("sum", 0, 1, 0, 3), ("sum", 1, 1, 1, 4), ("sum", 1, 0, 2, 4),
+    ("unit", 1, 1), ("near", 3), ("far", 2), ("unit", 1, 0), ("sum", 0, 0, 0, 4), ("sum", 1, 1, 3, 4),
+    ("sum", 1, 0, 1, 3), ("unit", 2, 1), ("near", 4), ("far", 3), ("unit", 2, 0), ("sum", 0, 1, 1, 4), ("near", 5),
+    ("sum", 1, 1, 2, 3), ("sum", 1, 0, 0, 3), ("unit", 3, 1), ("unit", 3, 0), ("sum", 1, 0, 4, 3),
+    ("sum", 1, 1, 0, 3), ("near", 6), ("sum", 1, 1, 1, 3), ("sum", 0, 0, 1, 3), ("sum", 1, 0, 3, 3),
+    ("sum", 0, 0, 0, 3), ("sum", 0, 1, 0, 2), ("far", 4), ("sum", 1, 1, 4, 3), ("sum", 1, 0, 2, 3), ("near", 7),
+    ("unit", 4, 1), ("far", 5), ("unit", 4, 0), ("sum", 0, 0, 2, 4), ("sum", 0, 1, 1, 3), ("far", 6),
+    ("sum", 0, 1, 2, 3), ("unit", 5, 1), ("unit", 5, 0), ("unit", 6, 1), ("unit", 6, 0), ("sum", 0, 1, 3, 4),
+    ("far", 7), ("sum", 1, 0, 4, 2), ("sum", 1, 1, 0, 2), ("sum", 1, 0, 0, 2), ("sum", 1, 1, 3, 3),
+    ("sum", 1, 0, 1, 2), ("unit", 7, 1), ("unit", 7, 0), ("sum", 0, 1, 4, 3), ("sum", 0, 0, 4, 4),
+    ("sum", 0, 0, 2, 3), ("sum", 0, 1, 1, 2), ("sum", 1, 1, 1, 2), ("sum", 0, 1, 0, 1), ("sum", 0, 0, 0, 2),
+    ("sum", 1, 0, 2, 2), ("sum", 1, 1, 2, 2), ("sum", 0, 1, 2, 2), ("sum", 0, 0, 1, 2), ("sum", 1, 0, 3, 2),
+    ("sum", 0, 0, 3, 3), ("sum", 0, 1, 3, 3), ("sum", 1, 1, 0, 1), ("sum", 1, 0, 0, 1), ("sum", 0, 1, 4, 2),
+    ("sum", 0, 0, 4, 3), ("sum", 1, 1, 3, 2), ("sum", 1, 0, 4, 1), ("sum", 0, 1, 1, 1), ("sum", 0, 0, 2, 2),
+    ("sum", 1, 0, 1, 1), ("sum", 0, 0, 0, 1), ("sum", 1, 1, 1, 1), ("sum", 0, 1, 2, 1), ("sum", 0, 0, 1, 1),
+    ("sum", 1, 1, 2, 1), ("sum", 1, 0, 2, 1), ("sum", 0, 1, 3, 2), ("sum", 0, 0, 3, 2), ("sum", 1, 0, 3, 1),
+    ("own", 1, 0), ("sum", 0, 0, 4, 2), ("sum", 1, 1, 4, 2), ("sum", 1, 1, 3, 1), ("sum", 0, 1, 4, 1),
+    ("sum", 0, 0, 2, 1), ("own", 0, 0), ("own", 1, 1), ("own", 0, 1), ("sum", 0, 1, 3, 1), ("sum", 0, 0, 3, 1),
+    ("sum", 0, 0, 4, 1), ("sum", 1, 1, 4, 1), ("own", 1, 2), ("own", 0, 2), ("own", 1, 3), ("own", 0, 3),
+    ("own", 1, 4), ("own", 0, 4),
 )
-MESH = pl.DeviceIdType.MESH
 
 
 def quantize(x):
@@ -62,7 +67,7 @@
         return ORDER
     order = []
     for j in range(n):
-        order += [("near", j), ("far", j), ("unit", j)]
+        order += [("near", j), ("far", j), ("unit", j, 0), ("unit", j, 1)]
     groups = range(len(groups_of(n)))
     for r in range(n // 2):
         for g in groups:
@@ -74,10 +79,12 @@
 
 def kernel(cfg, act_hbm, grad_hbm, rb_hbm, docs_hbm, out, act, grad, rb, docs, turn, gm, unit, gauge, sn, rn, cn, rcn,
            s2, r2, c2, rc2, in_sem, x_r, sib_r, m_r, m2_r, send_sem, *feats):
-    n, nx, nb, knz, per_half, factor = cfg
+    n, nx, nb, knz, halves, factor = cfg
     slots = act.shape[0]
     span = BLOCK // n
-    high = per_half * span
+    columns = sum(halves)
+    begins = (0, halves[0])
+    high = [wide * span for wide in halves]
     offsets, groups = offsets_of(n), groups_of(n)
     place = {o: j for j, o in enumerate(offsets)}
     dp = lax.axis_index("dp")
@@ -97,7 +104,7 @@
 
     peers = [{"dp": dp, "mp": sibling}]
     if nx > 1:
-        peers += [{"dp": dp, "mp": x_device(1)}, {"dp": dp, "mp": x_device(-1)}]
+        peers += [{"dp": dp, "mp": x_device(step)} for step in (1, 2, 3)]
     if n > 1:
         peers += [along(axis, step) for axis in (0, 1) for step in sorted({1, n - 1, 2 % n, (n - 2) % n} - {0})]
     barrier = pltpu.get_barrier_semaphore()
@@ -140,6 +147,8 @@
         if nx > 1:
             push(j, mp * nb, nb, right, 0, x_r.at[0, j]).start()
             push(j, mp * nb, nb, left, 0, x_r.at[1, j]).start()
+            if j < DIRECT:
+                push(j, mp * nb, nb, far, 0, x_r.at[2, j]).start()
         share(j, mp * nb, nb)
 
     for j in range(min(LEAD, n)):
@@ -151,16 +160,18 @@
     for d in range(1, docs.shape[1]):
         live = live + docs[0, d]
     keep = lax.broadcasted_iota(jnp.int32, (slots, BLOCK), 0) < live
-    for c in range(2 * per_half):
+    for c in range(columns):
         tile = grad[:, c * BLOCK:(c + 1) * BLOCK]
         gm[c] = jnp.where(keep, tile, jnp.zeros_like(tile))
 
     def near(j):
         if nx > 1:
             push(j, left * nb, nb, right, 0, x_r.at[0, j]).wait_recv()
-            push(j, left * nb, half, right, 0, x_r.at[2, j]).start()
+            if j >= DIRECT:
+                push(j, left * nb, half, right, 0, x_r.at[2, j]).start()
             push(j, right * nb, nb, left, 0, x_r.at[1, j]).wait_recv()
-            push(j, right * nb + half, half, left, 0, x_r.at[3, j]).start()
+            if j >= DIRECT:
+                push(j, right * nb + half, half, left, 0, x_r.at[3, j]).start()
         if j + LEAD < n:
             give(j + LEAD)
         if nx > 1:
@@ -168,15 +179,22 @@
             share(j, right * nb, nb)
 
     def from_far(j):
-        if nx > 1:
+        if nx > 1 and j < DIRECT:
+            push(j, far * nb, nb, far, 0, x_r.at[2, j]).wait_recv()
+            share(j, far * nb, nb)
+        elif nx > 1:
             push(j, far * nb, half, right, 0, x_r.at[2, j]).wait_recv()
             share(j, far * nb, half)
             push(j, far * nb + half, half, left, 0, x_r.at[3, j]).wait_recv()
             share(j, far * nb + half, half)
 
-    def products(j):
-        push(j, 0, nb * nx, sibling, 1, sib_r.at[j]).wait_recv()
-        for c in range(2 * per_half):
+    complete = set()
+
+    def products(j, h):
+        if j not in complete:
+            push(j, 0, nb * nx, sibling, 1, sib_r.at[j]).wait_recv()
+            complete.add(j)
+        for c in range(begins[h], begins[h] + halves[h]):
             lhs = jnp.concatenate([feats[j][rb[k, c]] for k in range(knz)], axis=0)
             sums = jnp.dot(lhs, gm[c], preferred_element_type=jnp.float32)
             unit[j, :, c] = sums.reshape(knz, span, BLOCK)
@@ -184,39 +202,40 @@
     def chunk(h, step, o):
         to_y, to_z = (step, o) if h == 0 else (o, step)
         k = lax.rem(at[0] + to_y + n, n)
-        return unit[place[to_z % n], k, h * per_half:(h + 1) * per_half].reshape(high, BLOCK)
-
-    plan, count = {}, 0
+        return unit[place[to_z % n], k, begins[h]:begins[h] + halves[h]].reshape(high[h], BLOCK)
+
+    plan, count, depth = {}, 0, 0
     for way in (0, 1):
         for g, group in enumerate(groups):
             for d in range(1, hops_of(n, way, g) + 1):
                 for h in (0, 1):
-                    plan[h, way, d, g] = (len(plan), count)
+                    plan[h, way, d, g] = (len(plan), count, depth)
                     count += len(group)
+                    depth += len(group) * high[h]
 
     def message(h, way, d, g):
-        index, first = plan[h, way, d, g]
+        index, first, start = plan[h, way, d, g]
         size = len(groups[g])
         to = along(h, 1 - 2 * way)
-        rows, scales = pl.ds(first * high, size * high), pl.ds(first, size)
+        rows, scales = pl.ds(start, size * high[h]), pl.ds(first, size)
         return (remote(cn.at[scales], rcn.at[scales], 4, m_r.at[index], to),
                 remote(sn.at[rows], rn.at[rows], 2, m_r.at[index], to))
 
     def add_arrived(values, h, way, d, g):
-        index, first = plan[h, way, d, g]
-        both = gauge.at[pl.ds(0, len(values))]
+        index, first, start = plan[h, way, d, g]
+        both = gauge.at[pl.ds(0, len(values)), pl.ds(0, high[h] // 2 + 1)]
         remote(both, both, 2, m_r.at[index], along(h, 1 - 2 * way)).wait_recv()
-        return [v + widen(rn[(first + i) * high:(first + i + 1) * high, :], rcn[first + i:first + i + 1, :])
+        return [v + widen(rn[start + i * high[h]:start + (i + 1) * high[h], :], rcn[first + i:first + i + 1, :])
                 for i, v in enumerate(values)]
 
     def step(h, way, g, d):
         values = [chunk(h, (1 - 2 * way) * d, o) for o in groups[g]]
         if d < hops_of(n, way, g):
             values = add_arrived(values, h, way, d + 1, g)
-        first = plan[h, way, d, g][1]
+        _, first, start = plan[h, way, d, g]
         for i, value in enumerate(values):
             q, scale = quantize(value)
-            sn[(first + i) * high:(first + i + 1) * high, :] = q
+            sn[start + i * high[h]:start + (i + 1) * high[h], :] = q
             cn[first + i:first + i + 1, :] = scale
         for copy in message(h, way, d, g):
             copy.start()
@@ -230,14 +249,15 @@
 
     def second(h, o):
         to = along(1 - h, target(h, o)[1])
-        row = pl.ds(h * n + o, 1)
+        row, rows = pl.ds(h * n + o, 1), pl.ds(begins[h] * span, high[h])
         return (remote(c2.at[row], rc2.at[row], 5, m2_r.at[h, o], to),
-                remote(s2.at[h, o], r2.at[h, o], 3, m2_r.at[h, o], to))
+                remote(s2.at[o, rows], r2.at[o, rows], 3, m2_r.at[h, o], to))
 
     def add_second(value, h, o):
-        both = gauge.at[pl.ds(0, 1)]
+        both = gauge.at[pl.ds(0, 1), pl.ds(0, high[h] // 2 + 1)]
         remote(both, both, 3, m2_r.at[h, o], along(1 - h, 1)).wait_recv()
-        return value + widen(r2[h, o], rc2[h * n + o:h * n + o + 1, :])
+        rows = slice(begins[h] * span, begins[h] * span + high[h])
+        return value + widen(r2[o, rows, :], rc2[h * n + o:h * n + o + 1, :])
 
     def own_step(h, g):
         values = [chunk(h, 0, o) for o in groups[g]]
@@ -249,10 +269,10 @@
                 if target(h, before)[0] == o:
                     value = add_second(value, h, before)
             if o == 0:
-                out[h * per_half:(h + 1) * per_half] = (value * factor).reshape(per_half, span, BLOCK)
+                out[begins[h]:begins[h] + halves[h]] = (value * factor).reshape(halves[h], span, BLOCK)
             else:
                 q, scale = quantize(value)
-                s2[h, o] = q
+                s2[o, begins[h] * span:begins[h] * span + high[h], :] = q
                 c2[h * n + o:h * n + o + 1, :] = scale
                 for copy in second(h, o):
                     copy.start()
@@ -271,7 +291,7 @@
     if n > 1:
         sent(sn, 2)
         sent(cn, 4)
-        sent(s2.at[:, pl.ds(1, n - 1)], 3)
+        sent(s2.at[pl.ds(1, n - 1)], 3)
         sent(rc2.at[pl.ds(0, 2 * (n - 1))], 5)
 
 
@@ -279,17 +299,18 @@
     slots = activations.shape[0]
     nb = activations.shape[1] // BLOCK
     columns, knz = row_blocks.shape
-    per_half = columns // 2
+    first = FIRST if columns == 14 else columns // 2 - 1
+    halves = (first, columns - first)
     factor = 1.0 / math.sqrt(slots * n * n)
     span = BLOCK // n
-    high = per_half * span
     sizes = [(len(group), hops_of(n, way, g)) for g, group in enumerate(groups_of(n)) for way in (0, 1) for h in (0, 1)]
     messages = max(1, sum(hops for _, hops in sizes))
     count = max(1, sum(hops * size for size, hops in sizes))
+    depth = max(16, columns * span * sum(hops * size for size, hops in sizes) // 2)
     dma = pltpu.SemaphoreType.DMA
     operands = (activations, out_grad, row_blocks.T, doc_lengths)
     return pl.pallas_call(
-        functools.partial(kernel, (n, nx, nb, knz, per_half, factor)),
+        functools.partial(kernel, (n, nx, nb, knz, halves, factor)),
         out_shape=jax.ShapeDtypeStruct((columns, span * knz // n, BLOCK), jnp.float32),
         in_specs=[pl.BlockSpec(memory_space=pl.ANY)] * 4,
         out_specs=pl.BlockSpec(memory_space=pltpu.VMEM),
@@ -301,13 +322,13 @@
             pltpu.VMEM((nb, BLOCK, slots), jnp.bfloat16),
             pltpu.VMEM((columns, slots, BLOCK), jnp.bfloat16),
             pltpu.VMEM((n, knz, columns, span, BLOCK), jnp.float32),
-            pltpu.VMEM((2, high // 2 + 1, BLOCK), jnp.float32),
-            pltpu.VMEM((count * high, BLOCK), jnp.int16),
-            pltpu.VMEM((count * high, BLOCK), jnp.int16),
+            pltpu.VMEM((2, max(halves) * span // 2 + 1, BLOCK), jnp.float32),
+            pltpu.VMEM((depth, BLOCK), jnp.int16),
+            pltpu.VMEM((depth, BLOCK), jnp.int16),
             pltpu.VMEM((count, BLOCK), jnp.float32),
             pltpu.VMEM((count, BLOCK), jnp.float32),
-            pltpu.VMEM((2, n, high, BLOCK), jnp.int16),
-            pltpu.VMEM((2, n, high, BLOCK), jnp.int16),
+            pltpu.VMEM((n, columns * span, BLOCK), jnp.int16),
+            pltpu.VMEM((n, columns * span, BLOCK), jnp.int16),
             pltpu.VMEM((2 * n, BLOCK), jnp.float32),
             pltpu.VMEM((2 * n, BLOCK), jnp.float32),
             dma((4,)),

time: 53.5 us -> 52.1 us (0.974)
  the two profiles are of different devices: /device:TPU:8 before, /device:TPU:1 now
where the time goes in v5:
time: 52.1 us; the launch traced here: 52 us
  Pallas kernels  51.3 us (98%)
  local copies, waits for them, and re-layouts  0.65 us (1%)
    pallas_call x1, Pallas kernels, shards(): pl.pallas_call(functools.partial(kernel, (n, nx, nb, knz, halves, factor)...  51.3 us

profile of v5, /device:TPU:1, one launch (start us, length us, event | category | flops | bytes accessed | tf_op | source)
XLA Modules:
  0.0 52.0 jit_solution(12850832485330902563)
XLA Ops:
  0.0 51.3 %shard_map.46 = f32[14,16,128]{2,1,0:T(8,128)S(1)} custom-call(bf16[256,512]{1,0:T(8,128)(2,1)} %act_hbm.1, bf16[256,1792]{1,0:T(8,128)(2,1)} %grad_hbm.1, s32[8,14]{1,0:T(8,128)} %bitcast.1, s32[1,4]{1,0:T(1,128)} %docs_hbm.1), custom_call_target="tpu_custom_call" | custom-call | tf_op jit(solution)/shard_map/pallas_call | solution.py:312
  51.3 0.6 %copy.6 = f32[14,16,128]{2,1,0:T(8,128)} copy(f32[14,16,128]{2,1,0:T(8,128)S(1)} %shard_map.46) | data formatting | bytes 229376

commit v6 on v5

v6 whole, which is shorter than its diff:
```python
import functools
import math

import jax
import jax.numpy as jnp
from jax import lax
from jax.experimental import pallas as pl
from jax.experimental.pallas import tpu as pltpu
from jax.sharding import PartitionSpec as P

BLOCK = 128
CORES = 2
TOP = 32700.0
TINY = 1e-33
PAIRS = True
JUMPS = (0, 1, 2, 2, 2)
FIRST = 6
MESH = pl.DeviceIdType.MESH
ORDER = (
    ("near", 0), ("unit", 0, 1), ("unit", 0, 0), ("near", 1), ("sum", 1, 0, 0, 4), ("sum", 1, 0, 4, 4),
    ("sum", 0, 1, 0, 3), ("sum", 1, 1, 1, 4), ("sum", 1, 0, 2, 4), ("unit", 1, 1), ("near", 2), ("unit", 1, 0),
    ("sum", 0, 0, 0, 4), ("sum", 1, 1, 3, 4), ("sum", 1, 0, 1, 3), ("unit", 2, 1), ("near", 3), ("unit", 2, 0),
    ("sum", 0, 1, 1, 4), ("sum", 1, 1, 2, 3), ("sum", 1, 0, 0, 3), ("unit", 3, 1), ("unit", 3, 0),
    ("sum", 1, 0, 4, 3), ("sum", 1, 1, 0, 3), ("sum", 1, 1, 1, 3), ("sum", 0, 0, 1, 3), ("sum", 1, 0, 3, 3),
    ("sum", 0, 0, 0, 3), ("sum", 0, 1, 0, 2), ("near", 4), ("sum", 1, 1, 4, 3), ("sum", 1, 0, 2, 3), ("unit", 4, 1),
    ("near", 5), ("unit", 4, 0), ("sum", 0, 0, 2, 4), ("sum", 0, 1, 1, 3), ("near", 6), ("sum", 0, 1, 2, 3),
    ("unit", 5, 1), ("unit", 5, 0), ("unit", 6, 1), ("unit", 6, 0), ("sum", 0, 1, 3, 4), ("near", 7),
    ("sum", 1, 0, 4, 2), ("sum", 1, 1, 0, 2), ("sum", 1, 0, 0, 2), ("sum", 1, 1, 3, 3), ("sum", 1, 0, 1, 2),
    ("unit", 7, 1), ("unit", 7, 0), ("sum", 0, 1, 4, 3), ("sum", 0, 0, 4, 4), ("sum", 0, 0, 2, 3),
    ("sum", 0, 1, 1, 2), ("sum", 1, 1, 1, 2), ("sum", 0, 1, 0, 1), ("sum", 0, 0, 0, 2), ("sum", 1, 0, 2, 2),
    ("sum", 1, 1, 2, 2), ("sum", 0, 1, 2, 2), ("sum", 0, 0, 1, 2), ("sum", 1, 0, 3, 2), ("sum", 0, 0, 3, 3),
    ("sum", 0, 1, 3, 3), ("sum", 1, 1, 0, 1), ("sum", 1, 0, 0, 1), ("sum", 0, 1, 4, 2), ("sum", 0, 0, 4, 3),
    ("sum", 1, 1, 3, 2), ("sum", 1, 0, 4, 1), ("sum", 0, 1, 1, 1), ("sum", 0, 0, 2, 2), ("sum", 1, 0, 1, 1),
    ("sum", 0, 0, 0, 1), ("sum", 1, 1, 1, 1), ("sum", 0, 1, 2, 1), ("sum", 0, 0, 1, 1), ("sum", 1, 1, 2, 1),
    ("sum", 1, 0, 2, 1), ("sum", 0, 1, 3, 2), ("sum", 0, 0, 3, 2), ("sum", 1, 0, 3, 1), ("own", 1, 0),
    ("sum", 0, 0, 4, 2), ("sum", 1, 1, 4, 2), ("sum", 1, 1, 3, 1), ("sum", 0, 1, 4, 1), ("sum", 0, 0, 2, 1),
    ("own", 0, 0), ("own", 1, 1), ("own", 0, 1), ("sum", 0, 1, 3, 1), ("sum", 0, 0, 3, 1), ("sum", 0, 0, 4, 1),
    ("sum", 1, 1, 4, 1), ("own", 1, 2), ("own", 0, 2), ("own", 1, 3), ("own", 0, 3), ("own", 1, 4), ("own", 0, 4),
)


def quantize(x):
    peak = jnp.maximum(jnp.max(jnp.abs(x), axis=0, keepdims=True), TINY)
    return jnp.round(x * (TOP / peak)).astype(jnp.int32).astype(jnp.int16), peak * (1.0 / TOP)


def widen(q, scale):
    return q.astype(jnp.int32).astype(jnp.float32) * scale


def offsets_of(n):
    return sorted(range(n), key=lambda o: (-min(o, n - o), o))


def groups_of(n):
    if not PAIRS:
        return [[o] for o in offsets_of(n)]
    return [[o for o in offsets_of(n) if min(o, n - o) == d] for d in range(n // 2, -1, -1)]


def hops_of(n, way, g):
    return n // 2 if way == g % 2 else n - 1 - n // 2


def order_of(n):
    if n == 8:
        return ORDER
    order = []
    for j in range(n):
        order += [("near", j), ("unit", j, 0), ("unit", j, 1)]
    groups = range(len(groups_of(n)))
    for r in range(n // 2):
        for g in groups:
            for h in (0, 1):
                order += [("sum", h, way, g, hops_of(n, way, g) - r)
                          for way in (g % 2, 1 - g % 2) if hops_of(n, way, g) > r]
    return order + [("own", h, g) for g in groups for h in (0, 1)]


def kernel(cfg, act_hbm, grad_hbm, rb_hbm, docs_hbm, out, act, grad, rb, docs, turn, gm, unit, gauge, sn, rn, cn, rcn,
           s2, r2, c2, rc2, in_sem, x_r, sib_r, m_r, last_r, m2_r, send_sem, *feats):
    n, nx, nb, knz, halves, factor = cfg
    slots = act.shape[0]
    span = BLOCK // n
    columns = sum(halves)
    begins = (0, halves[0])
    high = [wide * span for wide in halves]
    offsets, groups = offsets_of(n), groups_of(n)
    place = {o: j for j, o in enumerate(offsets)}
    dp = lax.axis_index("dp")
    mp = lax.axis_index("mp")
    at = (dp // n, lax.rem(dp, n))
    x, core = mp // CORES, lax.rem(mp, CORES)
    sibling = x * CORES + (1 - core)

    def along(axis, step):
        there = lax.rem(at[axis] + step + n, n)
        if axis == 0:
            return {"dp": there * n + at[1], "mp": mp}
        return {"dp": at[0] * n + there, "mp": mp}

    def x_device(step):
        return lax.rem(x + step + nx, nx) * CORES + core

    peers = [{"dp": dp, "mp": sibling}]
    if nx > 1:
        peers += [{"dp": dp, "mp": x_device(step)} for step in (1, 2, 3)]
    if n > 1:
        peers += [along(axis, step) for axis in (0, 1) for step in sorted({(sign * hop) % n for hop in set(JUMPS) for sign in (1, -1)} - {0})]
    barrier = pltpu.get_barrier_semaphore()
    for peer in peers:
        pl.semaphore_signal(barrier, inc=1, device_id=peer, device_id_type=MESH)

    loads = [pltpu.make_async_copy(a, b, in_sem.at[i])
             for i, (a, b) in enumerate(((act_hbm, act), (docs_hbm, docs), (rb_hbm, rb), (grad_hbm, grad)))]
    for load in loads:
        load.start()
    loads[0].wait()
    for b in range(nb):
        turn[b] = act[:, b * BLOCK:(b + 1) * BLOCK].T

    def cut(j):
        rows = pl.ds(pl.multiple_of(lax.rem(at[1] + offsets[j], n) * span, span), span)
        for b in range(nb):
            feats[j][mp * nb + b] = turn[b, rows, :]

    for j in range(n):
        cut(j)
    pl.semaphore_wait(barrier, len(peers))

    def remote(src, dst, send, recv, to):
        return pltpu.make_async_remote_copy(
            src_ref=src, dst_ref=dst, send_sem=send_sem.at[send], recv_sem=recv, device_id=to, device_id_type=MESH)

    def push(j, first, size, to, send, recv):
        piece = feats[j].at[pl.ds(first, size)]
        return remote(piece, piece, send, recv, {"dp": dp, "mp": to})

    def share(j, first, size):
        push(j, first, size, sibling, 1, sib_r.at[j]).start()

    others = [x_device(step) for step in (2, 1, 3)] if nx > 1 else []
    for j in range(n):
        for to in others:
            push(j, mp * nb, nb, to, 0, x_r.at[j]).start()
        share(j, mp * nb, nb)

    for load in loads[1:]:
        load.wait()
    live = docs[0, 0]
    for d in range(1, docs.shape[1]):
        live = live + docs[0, d]
    keep = lax.broadcasted_iota(jnp.int32, (slots, BLOCK), 0) < live
    for c in range(columns):
        tile = grad[:, c * BLOCK:(c + 1) * BLOCK]
        gm[c] = jnp.where(keep, tile, jnp.zeros_like(tile))

    def near(j):
        if nx > 1:
            push(j, 0, 3 * nb, sibling, 0, x_r.at[j]).wait_recv()
        for device in others:
            share(j, device * nb, nb)

    complete = set()

    def products(j, h):
        if j not in complete:
            push(j, 0, nb * nx, sibling, 1, sib_r.at[j]).wait_recv()
            complete.add(j)
        for c in range(begins[h], begins[h] + halves[h]):
            lhs = jnp.concatenate([feats[j][rb[k, c]] for k in range(knz)], axis=0)
            sums = jnp.dot(lhs, gm[c], preferred_element_type=jnp.float32)
            unit[j, :, c] = sums.reshape(knz, span, BLOCK)

    def chunk(h, step, o):
        to_y, to_z = (step, o) if h == 0 else (o, step)
        k = lax.rem(at[0] + to_y + n, n)
        return unit[place[to_z % n], k, begins[h]:begins[h] + halves[h]].reshape(high[h], BLOCK)

    plan, early, count, depth = {}, 0, 0, 0
    for way in (0, 1):
        for g, group in enumerate(groups):
            for d in range(1, hops_of(n, way, g) + 1):
                for h in (0, 1):
                    recv = last_r.at[h, g] if d == 1 else m_r.at[early]
                    early += d > 1
                    plan[h, way, d, g] = (recv, count, depth)
                    count += len(group)
                    depth += len(group) * high[h]

    def message(h, way, d, g):
        recv, first, start = plan[h, way, d, g]
        size = len(groups[g])
        to = along(h, 1 - 2 * way)
        rows, scales = pl.ds(start, size * high[h]), pl.ds(first, size)
        return (remote(cn.at[scales], rcn.at[scales], 4, recv, to),
                remote(sn.at[rows], rn.at[rows], 2, recv, to))

    def arrived(slots, h, send, recv):
        both = gauge.at[pl.ds(0, slots), pl.ds(0, high[h] // 2 + 1)]
        remote(both, both, send, recv, along(h, 1)).wait_recv()

    def add(values, h, way, d, g):
        _, first, start = plan[h, way, d, g]
        return [v + widen(rn[start + i * high[h]:start + (i + 1) * high[h], :], rcn[first + i:first + i + 1, :])
                for i, v in enumerate(values)]

    def step(h, way, g, d):
        values = [chunk(h, (1 - 2 * way) * d, o) for o in groups[g]]
        if d < hops_of(n, way, g):
            arrived(len(values), h, 2, plan[h, way, d + 1, g][0])
            values = add(values, h, way, d + 1, g)
        _, first, start = plan[h, way, d, g]
        for i, value in enumerate(values):
            q, scale = quantize(value)
            sn[start + i * high[h]:start + (i + 1) * high[h], :] = q
            cn[first + i:first + i + 1, :] = scale
        for copy in message(h, way, d, g):
            copy.start()

    def way_of(h, o):
        return 0 if o < n - o or (o == n - o and h == 0) else 1

    def target(h, o):
        hop = JUMPS[min(o, n - o)]
        return ((o - hop) % n, hop) if way_of(h, o) == 0 else ((o + hop) % n, -hop)

    def second(h, o):
        goals = sorted({target(h, b)[0] for b in range(1, n)})
        goal = m2_r.at[h, goals.index(target(h, o)[0])]
        to = along(1 - h, target(h, o)[1])
        row, rows = pl.ds(h * n + o, 1), pl.ds(begins[h] * span, high[h])
        return (remote(c2.at[row], rc2.at[row], 5, goal, to),
                remote(s2.at[o, rows], r2.at[o, rows], 3, goal, to))

    def own_step(h, g):
        values = [chunk(h, 0, o) for o in groups[g]]
        ways = [way for way in (0, 1) if hops_of(n, way, g) > 0]
        if ways:
            arrived(len(ways) * len(values), h, 2, last_r.at[h, g])
        for way in ways:
            values = add(values, h, way, 1, g)
        goals = sorted({target(h, b)[0] for b in range(1, n)})
        for value, o in zip(values, groups[g]):
            sources = [b for b in range(1, n) if target(h, b)[0] == o]
            if sources:
                arrived(len(sources), h, 3, m2_r.at[h, goals.index(o)])
            for b in sources:
                rows = slice(begins[h] * span, begins[h] * span + high[h])
                value = value + widen(r2[b, rows, :], rc2[h * n + b:h * n + b + 1, :])
            if o == 0:
                out[begins[h]:begins[h] + halves[h]] = (value * factor).reshape(halves[h], span, BLOCK)
            else:
                q, scale = quantize(value)
                s2[o, begins[h] * span:begins[h] * span + high[h], :] = q
                c2[h * n + o:h * n + o + 1, :] = scale
                for copy in second(h, o):
                    copy.start()

    run = {"near": near, "unit": products, "sum": step, "own": own_step}
    for op in order_of(n):
        run[op[0]](*op[1:])

    def sent(ref, i):
        remote(ref, ref, i, sib_r.at[0], {"dp": dp, "mp": sibling}).wait_send()

    for j in range(n):
        if nx > 1:
            sent(feats[j].at[pl.ds(0, 3 * nb)], 0)
        sent(feats[j].at[pl.ds(0, nb * nx)], 1)
    if n > 1:
        sent(sn, 2)
        sent(cn, 4)
        sent(s2.at[pl.ds(1, n - 1)], 3)
        sent(rc2.at[pl.ds(0, 2 * (n - 1))], 5)


def shards(n, nx, activations, out_grad, row_blocks, doc_lengths):
    slots = activations.shape[0]
    nb = activations.shape[1] // BLOCK
    columns, knz = row_blocks.shape
    first = FIRST if columns == 14 else columns // 2 - 1
    halves = (first, columns - first)
    factor = 1.0 / math.sqrt(slots * n * n)
    span = BLOCK // n
    sizes = [(len(group), hops_of(n, way, g)) for g, group in enumerate(groups_of(n)) for way in (0, 1) for h in (0, 1)]
    messages = max(1, sum(max(0, hops - 1) for _, hops in sizes))
    count = max(1, sum(hops * size for size, hops in sizes))
    depth = max(16, columns * span * sum(hops * size for size, hops in sizes) // 2)
    dma = pltpu.SemaphoreType.DMA
    operands = (activations, out_grad, row_blocks.T, doc_lengths)
    return pl.pallas_call(
        functools.partial(kernel, (n, nx, nb, knz, halves, factor)),
        out_shape=jax.ShapeDtypeStruct((columns, span * knz // n, BLOCK), jnp.float32),
        in_specs=[pl.BlockSpec(memory_space=pl.ANY)] * 4,
        out_specs=pl.BlockSpec(memory_space=pltpu.VMEM),
        scratch_shapes=[
            pltpu.VMEM(activations.shape, jnp.bfloat16),
            pltpu.VMEM(out_grad.shape, jnp.bfloat16),
            pltpu.SMEM(row_blocks.shape[::-1], jnp.int32),
            pltpu.SMEM(doc_lengths.shape, jnp.int32),
            pltpu.VMEM((nb, BLOCK, slots), jnp.bfloat16),
            pltpu.VMEM((columns, slots, BLOCK), jnp.bfloat16),
            pltpu.VMEM((n, knz, columns, span, BLOCK), jnp.float32),
            pltpu.VMEM((4, max(halves) * span // 2 + 1, BLOCK), jnp.float32),
            pltpu.VMEM((depth, BLOCK), jnp.int16),
            pltpu.VMEM((depth, BLOCK), jnp.int16),
            pltpu.VMEM((count, BLOCK), jnp.float32),
            pltpu.VMEM((count, BLOCK), jnp.float32),
            pltpu.VMEM((n, columns * span, BLOCK), jnp.int16),
            pltpu.VMEM((n, columns * span, BLOCK), jnp.int16),
            pltpu.VMEM((2 * n, BLOCK), jnp.float32),
            pltpu.VMEM((2 * n, BLOCK), jnp.float32),
            dma((4,)),
            dma((n,)),
            dma((n,)),
            dma((messages,)),
            dma((2, len(groups_of(n)))),
            dma((2, min(4, n))),
            dma((6,)),
        ] + [pltpu.VMEM((nb * nx * CORES, span, slots), jnp.bfloat16)] * n,
        compiler_params=pltpu.CompilerParams(
            collective_id=0, has_side_effects=True, vmem_limit_bytes=40 * 2**20),
    )(*(pltpu.with_memory_space_constraint(a, pltpu.HBM) for a in operands))


def solution(mesh):
    n = math.isqrt(mesh.shape["dp"])
    body = functools.partial(shards, n, mesh.shape["mp"] // CORES)
    in_specs = (P("dp", "mp"), P("dp", "mp"), P("mp", None), P("dp", None))
    return jax.shard_map(body, mesh=mesh, in_specs=in_specs, out_specs=P("mp", "dp", None), check_vma=False)
```

time: 52.1 us -> 50.2 us (0.964)
  Pallas kernels: 51.3 us -> 49.1 us
    pallas_call x1, Pallas kernels: 51.3 us -> 49.1 us  [shards(): pl.pallas_call(functools.partial(kernel, (n, nx, nb, knz, halves, factor)...]
where the time goes in v6:
time: 50.2 us; the launch traced here: 49.8 us
  Pallas kernels  49.1 us (98%)
  local copies, waits for them, and re-layouts  0.65 us (1%)
    pallas_call x1, Pallas kernels, shards(): pl.pallas_call(functools.partial(kernel, (n, nx, nb, knz, halves, factor)...  49.1 us

profile of v6, /device:TPU:1, one launch (start us, length us, event | category | flops | bytes accessed | tf_op | source)
XLA Modules:
  0.0 49.8 jit_solution(16549809701022496499)
XLA Ops:
  0.0 49.1 %shard_map.46 = f32[14,16,128]{2,1,0:T(8,128)S(1)} custom-call(bf16[256,512]{1,0:T(8,128)(2,1)} %act_hbm.1, bf16[256,1792]{1,0:T(8,128)(2,1)} %grad_hbm.1, s32[8,14]{1,0:T(8,128)} %bitcast.1, s32[1,4]{1,0:T(1,128)} %docs_hbm.1), custom_call_target="tpu_custom_call" | custom-call | tf_op jit(solution)/shard_map/pallas_call | solution.py:292
  49.1 0.6 %copy.6 = f32[14,16,128]{2,1,0:T(8,128)} copy(f32[14,16,128]{2,1,0:T(8,128)S(1)} %shard_map.46) | data formatting | bytes 229376

commit v7 on v6

--- a/solution.py
+++ b/solution.py
@@ -77,7 +77,7 @@
     return order + [("own", h, g) for g in groups for h in (0, 1)]
 
 
-def kernel(cfg, act_hbm, grad_hbm, rb_hbm, docs_hbm, out, act, grad, rb, docs, turn, gm, unit, gauge, sn, rn, cn, rcn,
+def kernel(cfg, act_hbm, grad_hbm, rb_hbm, docs_hbm, out, act, grad, rb, docs, spot, turn, gm, unit, gauge, sn, rn, cn, rcn,
            s2, r2, c2, rc2, in_sem, x_r, sib_r, m_r, last_r, m2_r, send_sem, *feats):
     n, nx, nb, knz, halves, factor = cfg
     slots = act.shape[0]
@@ -122,7 +122,7 @@
     def cut(j):
         rows = pl.ds(pl.multiple_of(lax.rem(at[1] + offsets[j], n) * span, span), span)
         for b in range(nb):
-            feats[j][mp * nb + b] = turn[b, rows, :]
+            feats[j][b] = turn[b, rows, :]
 
     for j in range(n):
         cut(j)
@@ -132,18 +132,18 @@
         return pltpu.make_async_remote_copy(
             src_ref=src, dst_ref=dst, send_sem=send_sem.at[send], recv_sem=recv, device_id=to, device_id_type=MESH)
 
-    def push(j, first, size, to, send, recv):
-        piece = feats[j].at[pl.ds(first, size)]
-        return remote(piece, piece, send, recv, {"dp": dp, "mp": to})
+    def push(j, first, size, there, to, send, recv):
+        return remote(feats[j].at[pl.ds(first, size)], feats[j].at[pl.ds(there, size)], send, recv, {"dp": dp, "mp": to})
 
     def share(j, first, size):
-        push(j, first, size, sibling, 1, sib_r.at[j]).start()
-
-    others = [x_device(step) for step in (2, 1, 3)] if nx > 1 else []
-    for j in range(n):
-        for to in others:
-            push(j, mp * nb, nb, to, 0, x_r.at[j]).start()
-        share(j, mp * nb, nb)
+        push(j, first, size, nx * nb + first, sibling, 1, sib_r.at[j]).start()
+
+    others = (2, 1, 3) if nx > 1 else ()
+    for j in range(n):
+        for step in others:
+            push(j, 0, nb, (nx - step) * nb, x_device(step), 0, x_r.at[j]).start()
+    for j in range(n):
+        share(j, 0, nb)
 
     for load in loads[1:]:
         load.wait()
@@ -152,23 +152,27 @@
         live = live + docs[0, d]
     keep = lax.broadcasted_iota(jnp.int32, (slots, BLOCK), 0) < live
     for c in range(columns):
+        for k in range(knz):
+            owner, block = lax.div(rb[k, c], nb), lax.rem(rb[k, c], nb)
+            part = lax.rem(lax.rem(owner, CORES) + core, CORES)
+            chip = lax.rem(lax.div(owner, CORES) - x + nx, nx)
+            spot[k, c] = (part * nx + chip) * nb + block
         tile = grad[:, c * BLOCK:(c + 1) * BLOCK]
         gm[c] = jnp.where(keep, tile, jnp.zeros_like(tile))
 
     def near(j):
         if nx > 1:
-            push(j, 0, 3 * nb, sibling, 0, x_r.at[j]).wait_recv()
-        for device in others:
-            share(j, device * nb, nb)
+            push(j, nb, 3 * nb, nb, sibling, 0, x_r.at[j]).wait_recv()
+            share(j, nb, 3 * nb)
 
     complete = set()
 
     def products(j, h):
         if j not in complete:
-            push(j, 0, nb * nx, sibling, 1, sib_r.at[j]).wait_recv()
+            push(j, 0, nb * nx, 0, sibling, 1, sib_r.at[j]).wait_recv()
             complete.add(j)
         for c in range(begins[h], begins[h] + halves[h]):
-            lhs = jnp.concatenate([feats[j][rb[k, c]] for k in range(knz)], axis=0)
+            lhs = jnp.concatenate([feats[j][spot[k, c]] for k in range(knz)], axis=0)
             sums = jnp.dot(lhs, gm[c], preferred_element_type=jnp.float32)
             unit[j, :, c] = sums.reshape(knz, span, BLOCK)
 
@@ -299,6 +303,7 @@
             pltpu.VMEM(out_grad.shape, jnp.bfloat16),
             pltpu.SMEM(row_blocks.shape[::-1], jnp.int32),
             pltpu.SMEM(doc_lengths.shape, jnp.int32),
+            pltpu.SMEM(row_blocks.shape[::-1], jnp.int32),
             pltpu.VMEM((nb, BLOCK, slots), jnp.bfloat16),
             pltpu.VMEM((columns, slots, BLOCK), jnp.bfloat16),
             pltpu.VMEM((n, knz, columns, span, BLOCK), jnp.float32),

time: 50.2 us -> 50.2 us (level)
  no operation moved by 1% of the time
where the time goes in v7:
time: 50.2 us; the launch traced here: 49.8 us
  Pallas kernels  49.1 us (98%)
  local copies, waits for them, and re-layouts  0.65 us (1%)
    pallas_call x1, Pallas kernels, shards(): pl.pallas_call(functools.partial(kernel, (n, nx, nb, knz, halves, factor)...  49.1 us

profile of v7, /device:TPU:1, one launch (start us, length us, event | category | flops | bytes accessed | tf_op | source)
XLA Modules:
  0.0 49.8 jit_solution(9883310102941892711)
XLA Ops:
  0.0 49.1 %shard_map.46 = f32[14,16,128]{2,1,0:T(8,128)S(1)} custom-call(bf16[256,512]{1,0:T(8,128)(2,1)} %act_hbm.1, bf16[256,1792]{1,0:T(8,128)(2,1)} %grad_hbm.1, s32[8,14]{1,0:T(8,128)} %bitcast.1, s32[1,4]{1,0:T(1,128)} %docs_hbm.1), custom_call_target="tpu_custom_call" | custom-call | tf_op jit(solution)/shard_map/pallas_call | solution.py:296
  49.1 0.6 %copy.6 = f32[14,16,128]{2,1,0:T(8,128)} copy(f32[14,16,128]{2,1,0:T(8,128)S(1)} %shard_map.46) | data formatting | bytes 229376
